TPU v7x, 256 devices: a whole 4x4x8 slice. The times are simulated.
256 devices in a mesh: src: 32 (over y, x, z_hi), tgt: 8 (over z_lo, core).
Axes of the slice: x: 4, y: 4, z: 8 (z_hi: 2, z_lo: 4; z = z_hi * 4 + z_lo), core: 2. Of those that a mesh axis runs over, the one named last changes fastest.
Arguments:
- source_bands: bfloat16 [32, 128, 128, 128], P('src', 'tgt'), may hold values from -6 to 6
- target_bands: bfloat16 [8, 128, 128, 128], P('tgt', 'src'), may hold values from -6 to 6
Outputs:
- exchange_field: float32 [8, 128, 128, 128], P('tgt', 'src')
All inputs are finite; a program needn't handle non-finite values.
Results may differ from a plain program's by a relative error of at most 0.033.
Values may be sent and summed in bfloat16 or wider, within the bound.
No kernel may reach another device: no remote copies, remote signals or barrier semaphores. Data moves between devices by JAX's collectives and lax.ppermute only.
A program may use at most 128 MiB of HBM per device.

v0:
```python
import math

import jax
import jax.numpy as jnp
from jax import lax
from jax.sharding import PartitionSpec as P

NX = 128
NY = 128
NZ = 128


FRACTION = 0.25
CELL = 59.2
ALONG_Z = "...xyz,zk->...xyk"
ALONG_Y = "...xyz,yk->...xkz"
ALONG_X = "...xyz,xk->...kyz"


def tables(points):
    counter = jnp.arange(points, dtype=jnp.int32)
    product = counter[:, None] * counter[None, :] % points
    angles = 2.0 * math.pi / points * product.astype(jnp.float32)
    return (jnp.cos(angles).astype(jnp.bfloat16), jnp.sin(angles).astype(jnp.bfloat16))


def wave_squares(points):
    counter = jnp.arange(points, dtype=jnp.int32)
    wrapped = jnp.where(counter < points // 2, counter, counter - points)
    frequency = 2.0 * math.pi / CELL * wrapped.astype(jnp.float32)
    return frequency * frequency


def coulomb_kernel():
    wave_sq = (
        wave_squares(NX)[:, None, None]
        + wave_squares(NY)[None, :, None]
        + wave_squares(NZ)[None, None, :]
    )
    radius = CELL * (3.0 / (4.0 * math.pi)) ** (1.0 / 3.0)
    safe_sq = jnp.where(wave_sq > 0, wave_sq, 1.0)
    magnitude = jnp.sqrt(safe_sq)
    values = jnp.where(
        wave_sq > 0,
        4.0 * math.pi * (1.0 - jnp.cos(magnitude * radius)) / safe_sq,
        2.0 * math.pi * radius * radius,
    )
    return values / (NX * NY * NZ)


def contract(operand, table, pattern):
    return jnp.einsum(pattern, operand, table, preferred_element_type=jnp.float32)


def rotate(real_part, imag_part, cos_table, sin_table, pattern, direction):
    new_real = contract(real_part, cos_table, pattern) + direction * contract(
        imag_part, sin_table, pattern
    )
    new_imag = contract(imag_part, cos_table, pattern) - direction * contract(
        real_part, sin_table, pattern
    )
    return (new_real.astype(jnp.bfloat16), new_imag.astype(jnp.bfloat16))


def forward_planes(density):
    cos_y, sin_y = tables(NY)
    cos_z, sin_z = tables(NZ)
    real_part = contract(density, cos_z, ALONG_Z).astype(jnp.bfloat16)
    imag_part = (-contract(density, sin_z, ALONG_Z)).astype(jnp.bfloat16)
    return rotate(real_part, imag_part, cos_y, sin_y, ALONG_Y, 1.0)


def on_device(source_bands, target_bands):
    target_whole = lax.all_gather(target_bands, "src", axis=1, tiled=True)[0]
    shard_piece = lax.all_gather(source_bands, "tgt", axis=1, tiled=True)
    density = (shard_piece.astype(jnp.float32) * target_whole.astype(jnp.float32)[None]).astype(
        jnp.bfloat16
    )
    real_part, imag_part = forward_planes(density)
    stacked = jnp.stack([shard_piece, real_part, imag_part])
    source_whole = stacked[0]
    real_part = stacked[1]
    imag_part = stacked[2]
    cos_x, sin_x = tables(NX)
    cos_y, sin_y = tables(NY)
    cos_z, sin_z = tables(NZ)
    real_part, imag_part = rotate(real_part, imag_part, cos_x, sin_x, ALONG_X, 1.0)
    kernel = coulomb_kernel()
    real_part = (real_part.astype(jnp.float32) * kernel).astype(jnp.bfloat16)
    imag_part = (imag_part.astype(jnp.float32) * kernel).astype(jnp.bfloat16)
    real_part, imag_part = rotate(real_part, imag_part, cos_z, sin_z, ALONG_Z, -1.0)
    real_part, imag_part = rotate(real_part, imag_part, cos_y, sin_y, ALONG_Y, -1.0)
    potential = contract(real_part, cos_x, ALONG_X) - contract(imag_part, sin_x, ALONG_X)
    band_term = -FRACTION * jnp.sum(source_whole.astype(jnp.float32) * potential, axis=0)
    own_rows = lax.psum_scatter(
        band_term.astype(jnp.bfloat16), "src", scatter_dimension=0, tiled=True
    ).astype(jnp.float32)
    return own_rows[None]


def solution(mesh):
    in_specs = (P("src", "tgt", None, None), P("tgt", "src", None, None))
    out_specs = P("tgt", "src", None, None)
    return jax.shard_map(
        on_device, mesh=mesh, in_specs=in_specs, out_specs=out_specs, check_vma=False
    )
```

profile of v0, /device:TPU:32, one launch (start us, length us, event | category | flops | bytes accessed | tf_op | source)
XLA Modules:
  0.0 655.9 jit_solution(6490526609697007577)
XLA Ops:
  6.5 0.0 all-gather.3.cloned.1.call-start
  6.5 2.2 copy.26
  8.7 0.0 all-gather.3.cloned.1.call-update
  8.7 0.0 all-gather.5.cloned.1.call-start
  8.8 0.7 all-gather.5.cloned.1.call-update
  9.5 0.0 reduce-scatter.2.cloned.1.call-start
  9.6 0.3 fusion.195
  9.8 0.3 fusion.193
  10.1 0.1 broadcast_add_fusion
  10.2 54.1 %all-gather.3.cloned.1.call-done = bf16[1,128,128,128]{3,1,2,0:T(8,128)(2,1)} async-done(((bf16[1,16,128,128]{3,1,2,0:T(8,128)(2,1)}), bf16[1,128,128,128]{3,1,2,0:T(8,128)(2,1)}) %all-gather.3.cloned.1.call-update) | async-done | bytes 4194320 | tf_op jit(solution)/shard_map/all_gather | solution.py:75
  64.3 115.3 %all-gather.5.cloned.1.call-done = bf16[1,128,128,128]{3,2,0,1:T(8,128)(2,1)} async-done(((bf16[1,4,128,128]{3,2,0,1:T(8,128)(2,1)}), bf16[1,128,128,128]{3,2,0,1:T(8,128)(2,1)}) %all-gather.5.cloned.1.call-update) | async-done | bytes 4194320 | tf_op jit(solution)/shard_map/all_gather | solution.py:74
  179.6 6.5 fusion.22
  186.2 8.8 %negate_convert_fusion = bf16[128,128,128]{2,1,0:T(8,128)(2,1)S(1)} fusion(bf16[128,128,128]{2,0,1:T(8,128)(2,1)S(1)} %fusion.22), kind=kOutput, calls=%fused_computation.29 | convolution fusion | flops 541310976 | bytes 8388608 | tf_op jit(solution)/shard_map/...xyz,zk->...xyk/dot_general | solution.py:52
  194.9 8.5 %fusion.51 = bf16[128,128,128]{2,1,0:T(8,128)(2,1)S(1)} fusion(bf16[128,128,128]{2,0,1:T(8,128)(2,1)S(1)} %fusion.22), kind=kOutput, calls=%fused_computation.60 | convolution fusion | flops 539213824 | bytes 8388608 | tf_op jit(solution)/shard_map/...xyz,zk->...xyk/dot_general | solution.py:52
  203.5 1.5 fusion.89
  204.9 1.7 fusion.92
  206.6 1.5 fusion.14
  208.1 6.6 %fusion.35 = f32[128,128,128]{2,0,1:T(8,128)} fusion(bf16[128,128,128]{2,1,0:T(8,128)(2,1)S(1)} %fusion.14), kind=kOutput, calls=%fused_computation.50 | convolution fusion | flops 537116672 | bytes 12582912 | tf_op jit(solution)/shard_map/...xyz,xk->...kyz/dot_general | solution.py:52
  214.7 3.4 fusion.33
  218.1 1.5 fusion.13
  219.6 0.0 copy-start
  219.6 43.3 %multiply_convert_fusion = bf16[128,128,128]{2,0,1:T(8,128)(2,1)S(1)} fusion(f32[128,128,128]{2,0,1:T(8,128)S(1)} %fusion.33, f32[128]{0:T(128)S(1)} %fusion.96, f32[128,128]{0,1:T(8,128)S(1)} %broadcast_add_fusion, bf16[128,128,128]{2,1,0:T(8,128)(2,1)S(1)} %fusion.13, bf16[128,128,1]{0,1,2:T(8,128)(2,1)S(1)} %fusion.193), kind=kOutput, calls=%fused_computation.23 | convolution fusion | flops 566231040 | bytes 16876032 | tf_op jit(solution)/shard_map/...xyz,xk->...kyz/dot_general | solution.py:52
  262.8 0.0 copy-done
  262.8 0.0 slice-start
  262.8 8.6 %fusion.27 = f32[128,128,128]{2,1,0:T(8,128)S(1)} fusion(bf16[128,128,128]{2,0,1:T(8,128)(2,1)S(1)} %multiply_convert_fusion), kind=kOutput, calls=%fused_computation.42 | convolution fusion | flops 537116672 | bytes 12582912 | tf_op jit(solution)/shard_map/...xyz,zk->...xyk/dot_general | solution.py:52
  271.4 0.0 slice-start.1
  271.4 0.0 copy-start.1
  271.4 8.8 %fusion.25 = f32[128,128,128]{2,1,0:T(8,128)S(1)} fusion(bf16[128,128,128]{2,0,1:T(8,128)(2,1)S(1)} %multiply_convert_fusion), kind=kOutput, calls=%fused_computation.40 | convolution fusion | flops 537116672 | bytes 12582912 | tf_op jit(solution)/shard_map/...xyz,zk->...xyk/dot_general | solution.py:52
  280.2 0.0 slice-done
  280.2 0.0 slice-done.1
  280.2 0.0 copy-done.1
  280.2 42.7 %multiply_convert_fusion.1 = bf16[128,128,128]{2,0,1:T(8,128)(2,1)S(1)} fusion(f32[128,128,128]{2,0,1:T(8,128)S(1)} %bitcast.87, f32[128]{0:T(128)S(1)} %fusion.96, f32[128,128]{0,1:T(8,128)S(1)} %broadcast_add_fusion, bf16[128,128,128]{2,1,0:T(8,128)(2,1)S(1)} %copy-done.1, bf16[128,128,1]{0,1,2:T(8,128)(2,1)S(1)} %fusion.195), kind=kOutput, calls=%fused_computation.25 | convolution fusion | flops 566231040 | bytes 16876032 | tf_op jit(solution)/shard_map/...xyz,xk->...kyz/dot_general | solution.py:52
  323.0 8.9 %add_convert_fusion = bf16[128,128,128]{2,1,0:T(8,128)(2,1)S(1)} fusion(f32[128,128,128]{2,1,0:T(8,128)S(1)} %fusion.27, bf16[128,128,128]{2,0,1:T(8,128)(2,1)S(1)} %multiply_convert_fusion.1), kind=kOutput, calls=%fused_computation.22 | convolution fusion | flops 543408128 | bytes 16777216 | tf_op jit(solution)/shard_map/...xyz,zk->...xyk/dot_general | solution.py:52
  331.9 1.5 fusion.86
  333.4 5.1 fusion.72
  338.5 9.0 %subtract_convert_fusion = bf16[128,128,128]{2,1,0:T(8,128)(2,1)S(1)} fusion(f32[128,128,128]{2,1,0:T(8,128)S(1)} %fusion.25, bf16[128,128,128]{2,0,1:T(8,128)(2,1)S(1)} %multiply_convert_fusion.1), kind=kOutput, calls=%fused_computation.21 | convolution fusion | flops 543408128 | bytes 16777216 | tf_op jit(solution)/shard_map/...xyz,zk->...xyk/dot_general | solution.py:52
  347.4 1.5 fusion.74
  348.9 4.9 fusion.83
  353.8 10.2 %fusion.16 = f32[128,128,128]{2,0,1:T(8,128)S(1)} fusion(f32[128,128,128]{2,0,1:T(8,128)S(1)} %fusion.74, f32[128,128,128]{2,0,1:T(8,128)S(1)} %fusion.86), kind=kOutput, calls=%fused_computation.33 | convolution fusion | flops 543408128 | bytes 25165824 | tf_op jit(solution)/shard_map/...xyz,xk->...kyz/dot_general | solution.py:52
  364.0 20.5 %fusion.21 = bf16[128,128,128]{2,0,1:T(8,128)(2,1)} fusion(f32[128,128,128]{2,0,1:T(8,128)S(1)} %fusion.16, bf16[1,128,128,128]{3,1,2,0:T(8,128)(2,1)} %all-gather.3.cloned.1.call-done, f32[128,128,128]{2,0,1:T(8,128)} %fusion.72, f32[128,128,128]{2,0,1:T(8,128)} %fusion.83), kind=kOutput, calls=%fused_computation.36 | convolution fusion | flops 553893888 | bytes 33554432 | tf_op jit(solution)/shard_map/...xyz,xk->...kyz/dot_general | solution.py:52
  384.5 6.8 %copy.49 = bf16[128,128,128]{2,1,0:T(8,128)(2,1)} copy(bf16[128,128,128]{2,0,1:T(8,128)(2,1)} %fusion.21) | data formatting | bytes 8388608 | tf_op jit(solution)/shard_map/convert_element_type | solution.py:96
  391.3 0.0 reduce-scatter.2.cloned.1.call-update
  391.4 256.0 %reduce-scatter.2.cloned.1.call-done = bf16[4,128,128]{2,1,0:T(8,128)(2,1)} async-done(((bf16[128,128,128]{2,1,0:T(8,128)(2,1)}), bf16[4,128,128]{2,1,0:T(8,128)(2,1)}) %reduce-scatter.2.cloned.1.call-update) | async-done | bytes 131088 | tf_op jit(solution)/shard_map/reduce_scatter | solution.py:95
  647.4 1.6 bitcast_convert_fusion
  (2 shorter events, 0.0 us)
Async XLA Ops:
  6.5 57.8 %all-gather.3.cloned.1.call-start = ((), (), s32[]{:S(2)}) async-start(), calls=%async_computation.1 | async-start | bytes 4718592 | tf_op jit(solution)/shard_map/all_gather | solution.py:75
  8.7 170.9 %all-gather.5.cloned.1.call-start = ((), (), s32[]{:S(2)}) async-start(), calls=%async_computation.2 | async-start | bytes 4325376 | tf_op jit(solution)/shard_map/all_gather | solution.py:74
  9.5 637.9 %reduce-scatter.2.cloned.1.call-start = ((), (), s32[]{:S(2)}) async-start(), calls=%async_computation.3 | async-start | bytes 4325376 | tf_op jit(solution)/shard_map/reduce_scatter | solution.py:95
  219.6 43.3 %copy-start = (bf16[128,128,128]{2,1,0:T(8,128)(2,1)}, bf16[128,128,128]{2,1,0:T(8,128)(2,1)S(1)}, u32[]{:S(2)}) copy-start(bf16[128,128,128]{2,1,0:T(8,128)(2,1)S(1)} %fusion.13) | copy-start | bytes 12582916
  262.8 17.4 %slice-start = ((s8[8388608]{0:T(1024)(128)(4,1)}), s8[4194304]{0:T(1024)(128)(4,1)S(1)}, s32[]{:S(2)}) async-start(s8[8388608]{0:T(1024)(128)(4,1)} %bitcast.86), calls=%async_computation.4 | async-start | bytes 8388608
  271.4 8.8 %slice-start.1 = ((s8[8388608]{0:T(1024)(128)(4,1)}), s8[4194304]{0:T(1024)(128)(4,1)S(1)}, s32[]{:S(2)}) async-start(s8[8388608]{0:T(1024)(128)(4,1)} %bitcast.86), calls=%async_computation.5 | async-start | bytes 8388608
  271.4 8.8 %copy-start.1 = (bf16[128,128,128]{2,1,0:T(8,128)(2,1)S(1)}, bf16[128,128,128]{2,1,0:T(8,128)(2,1)}, u32[]{:S(2)}) copy-start(bf16[128,128,128]{2,1,0:T(8,128)(2,1)} %copy-done) | copy-start | bytes 12582916
Sparse Core Ops, SparseCore 0:
  9.1 55.1 all-gather.2
  67.7 111.8 all-gather.4
  391.5 255.8 reduce-scatter.1
where the time goes:
time: 665 us; the launch traced here: 656 us
  waiting for transfers between devices  426 us (64%)
  matrix products  198 us (30%)
  between operations  13.6 us (2%)
  local copies, waits for them, and re-layouts  9.03 us (1%)
  other arithmetic  8.76 us (1%)
    reduce_scatter x1, waiting for transfers between devices, on_device(): lax.psum_scatter(band_term.astype(jnp.bfloat16), 'src', scatter_dimension...  256 us
    dot_general x20, matrix products, contract(): jnp.einsum(pattern, operand, table, preferred_element_type=jnp.float32)  198 us
    all_gather x1, waiting for transfers between devices, on_device(): target_whole = lax.all_gather(target_bands, 'src', axis=1, tiled=True)[0]  115 us
    all_gather x1, waiting for transfers between devices, on_device(): shard_piece = lax.all_gather(source_bands, 'tgt', axis=1, tiled=True)  54.1 us
  transfers between devices with their start and end apart: 3, of which 3 were waited for; matrix products, arithmetic and copies ran while one was open for 0% of the time, Pallas kernels for 0%

commit v1 on v0

v1 whole, which is shorter than its diff:
```python
import functools
import math

import jax
import jax.numpy as jnp
import ml_dtypes
import numpy as np
from jax import lax
from jax.experimental import pallas as pl
from jax.experimental.pallas import tpu as pltpu
from jax.sharding import Mesh
from jax.sharding import PartitionSpec as P

N = 128
HALF = N // 2
KEPT = HALF + 1
SLAB = 16
PLANES = KEPT + 1
SHARE = PLANES // 2
CHUNK = 11
FIRST_PITCH = N + 8
LAST_PITCH = SLAB + 8
FRACTION = 0.25
CELL = 59.2
MIB = 1024 * 1024
BF16 = jnp.bfloat16
F32 = jnp.float32


def tables():
    counter = np.arange(N)
    angles = (2.0 * math.pi / N) * (counter[:, None] * counter[None, :] % N)
    cos = np.cos(angles)
    sin = np.sin(angles)
    first = np.concatenate([cos[:KEPT], -sin[1:HALF]], axis=0)
    weight = np.full(N, 2.0)
    weight[0] = weight[HALF] = 1.0
    last = -FRACTION * np.concatenate(
        [cos[:, :KEPT] * weight[None, :KEPT], -2.0 * sin[:, 1:HALF]], axis=1
    )
    forward = np.block([[cos, -sin], [sin, cos]])
    inverse = np.block([[cos, sin], [-sin, cos]])
    x = np.arange(N).reshape(4, 2, 2, 2, 4)
    order = np.concatenate([x[:, :, :, c][:, [c, 1 - c]].reshape(HALF) for c in range(2)])
    both = np.concatenate([order, order + N])
    every = (first, last, forward, inverse, forward.T[:, both], inverse.T[both, :])
    return [np.asarray(t, np.float32).astype(ml_dtypes.bfloat16) for t in every]


def coulomb_kernel():
    counter = np.arange(N)
    wrapped = np.where(counter < HALF, counter, counter - N)
    wave = (2.0 * math.pi / CELL * wrapped) ** 2
    wave_sq = wave[:KEPT, None, None] + wave[None, :, None] + wave[None, None, :]
    radius = CELL * (3.0 / (4.0 * math.pi)) ** (1.0 / 3.0)
    safe_sq = np.where(wave_sq > 0, wave_sq, 1.0)
    values = np.where(
        wave_sq > 0,
        4.0 * math.pi * (1.0 - np.cos(np.sqrt(safe_sq) * radius)) / safe_sq,
        2.0 * math.pi * radius * radius,
    )
    values = values / N**3
    values = np.concatenate([values, np.zeros((1, N, N))]).astype(np.float32)
    return values.astype(ml_dtypes.bfloat16).reshape(2, SHARE, N, N)


def dot(left, right):
    return jnp.dot(left, right, preferred_element_type=F32)


def forward_kernel(count, info, *refs):
    pieces, t_all, first, lane_fwd, mine, give = refs[: 2 * count], *refs[2 * count : 2 * count + 5]
    wide, pq, o_buf, out_sem = refs[2 * count + 5 :]
    core = info[0]
    zeros = jnp.zeros((SLAB, N), BF16)
    pq[0:SLAB, N:] = zeros
    pq[HALF * SLAB : KEPT * SLAB, N:] = zeros
    pq[KEPT * SLAB :, 0:N] = zeros
    pq[KEPT * SLAB :, N:] = zeros
    stores = []
    for i in range(count):
        t_at = [4 * info[1 + i] + 2 * core, 4 * info[1 + i] + 2 * (1 - core)]
        for j in range(0, SLAB, 2):
            density = jnp.concatenate(
                [
                    pieces[2 * i + m // 8][m % 8] * t_all[t_at[m // 8] + m // 4 % 2, m % 4]
                    for m in (j, j + 1)
                ],
                axis=1,
            )
            out = dot(first[...], density)
            wide[pl.ds(j * FIRST_PITCH, N)] = out[:, :N]
            wide[pl.ds((j + 1) * FIRST_PITCH, N)] = out[:, N:]
        for k in range(KEPT):
            rows = pl.ds(k * SLAB, SLAB)
            pq[rows, 0:N] = wide[pl.ds(k, SLAB, stride=FIRST_PITCH)].astype(BF16)
            if 0 < k < HALF:
                pq[rows, N:] = wide[pl.ds(HALF + k, SLAB, stride=FIRST_PITCH)].astype(BF16)
        for part in range(PLANES // CHUNK):
            out = dot(pq[pl.ds(part * CHUNK * SLAB, CHUNK * SLAB)], lane_fwd[...]).astype(BF16)
            half, ks = part // 3, pl.ds(part % 3 * CHUNK, CHUNK)
            o_buf[i, half, ks, 0] = out[:, :N].reshape(CHUNK, SLAB, N)
            o_buf[i, half, ks, 1] = out[:, N:].reshape(CHUNK, SLAB, N)
        stores.append(pltpu.make_async_copy(o_buf.at[i, core], mine.at[i], out_sem.at[i, 0]))
        stores.append(pltpu.make_async_copy(o_buf.at[i, 1 - core], give.at[i], out_sem.at[i, 1]))
        stores[-1].start()
        stores[-2].start()
    for copy in stores:
        copy.wait()


HBM = pl.BlockSpec(memory_space=pltpu.HBM)
VMEM = pl.BlockSpec(memory_space=pltpu.VMEM)
SMEM = pl.BlockSpec(memory_space=pltpu.SMEM)


def forward(info, pieces, t_all, consts):
    count = len(pieces) // 2
    out = jax.ShapeDtypeStruct((count, SHARE, 2, SLAB, N), BF16)
    return pl.pallas_call(
        functools.partial(forward_kernel, count),
        out_shape=(out, out),
        in_specs=[SMEM] + [VMEM] * (2 * count + 3),
        out_specs=(HBM, HBM),
        scratch_shapes=[
            pltpu.VMEM((SLAB * FIRST_PITCH, N), F32),
            pltpu.VMEM((PLANES * SLAB, 2 * N), BF16),
            pltpu.VMEM((count, 2, SHARE, 2, SLAB, N), BF16),
            pltpu.SemaphoreType.DMA((count, 2)),
        ],
        compiler_params=pltpu.CompilerParams(vmem_limit_bytes=8 * MIB),
        cost_estimate=pl.CostEstimate(
            flops=count * 3500 * 256 * 256, bytes_accessed=count << 21, transcendentals=0
        ),
        name="forward",
    )(info, *pieces, t_all, consts[0], consts[2])


STEPS = ((0, 1, 7), (2, 6), (3, 5, 4))


def middle_kernel(info, *refs):
    own, come = refs[:3], refs[3:6]
    k_hbm, row_fwd, row_inv, mine, give, spec, done, k_buf, in_sem, k_sem, out_sem = refs[6:]
    core, place = info[0], info[1]
    parts = SHARE // CHUNK

    def loads(part):
        ks = pl.ds(part * CHUNK, CHUNK)
        copies = [pltpu.make_async_copy(k_hbm.at[core, ks], k_buf.at[ks], k_sem.at[part])]
        for step, distances in enumerate(STEPS):
            for i, distance in enumerate(distances):
                at = lax.rem(place + 8 - distance, 8)
                for side, (refs_of, row) in enumerate(((own, core), (come, 1 - core))):
                    rows = pl.ds(pl.multiple_of(row * HALF + at % 4 * SLAB, SLAB), SLAB)
                    copies.append(
                        pltpu.make_async_copy(
                            refs_of[step].at[i, ks],
                            spec.at[at // 4, ks, :, rows],
                            in_sem.at[part, distance, side],
                        )
                    )
        return copies

    def stores(part):
        ks = pl.ds(part * CHUNK, CHUNK)
        copies = []
        for side, (ref, row) in enumerate(((mine, core), (give, 1 - core))):
            rows = pl.ds(pl.multiple_of(row * HALF, HALF), HALF)
            copies.append(
                pltpu.make_async_copy(
                    done.at[:, ks, :, rows], ref.at[:, ks], out_sem.at[part, side]
                )
            )
        return copies

    for part in range(parts):
        for copy in loads(part):
            copy.start()
    for part in range(parts):
        for copy in loads(part):
            copy.wait()
        for k in range(part * CHUNK, (part + 1) * CHUNK):
            both = jnp.concatenate(
                [spec[0, k].reshape(2 * N, N), spec[1, k].reshape(2 * N, N)], axis=1
            )
            out = dot(row_fwd[...], both)
            scale = jnp.concatenate([k_buf[k], k_buf[k]], axis=1).astype(F32)
            out = jnp.concatenate([out[:N] * scale, out[N:] * scale], axis=0).astype(BF16)
            out = dot(row_inv[...], out).astype(BF16)
            done[0, k] = out[:, :N].reshape(2, N, N)
            done[1, k] = out[:, N:].reshape(2, N, N)
        for copy in stores(part):
            copy.start()
    for part in range(parts):
        for copy in stores(part):
            copy.wait()


def middle(info, own, come, consts):
    out = jax.ShapeDtypeStruct((2, SHARE, 2, HALF, N), BF16)
    return pl.pallas_call(
        middle_kernel,
        out_shape=(out, out),
        in_specs=[SMEM] + [HBM] * 7 + [VMEM] * 2,
        out_specs=(HBM, HBM),
        scratch_shapes=[
            pltpu.VMEM((2, SHARE, 2, N, N), BF16),
            pltpu.VMEM((2, SHARE, 2, N, N), BF16),
            pltpu.VMEM((SHARE, N, N), BF16),
            pltpu.SemaphoreType.DMA((3, 8, 2)),
            pltpu.SemaphoreType.DMA((3,)),
            pltpu.SemaphoreType.DMA((3, 2)),
        ],
        compiler_params=pltpu.CompilerParams(vmem_limit_bytes=14 * MIB),
        cost_estimate=pl.CostEstimate(
            flops=2 * 17000 * 256 * 256, bytes_accessed=11 << 20, transcendentals=0
        ),
        name="middle",
    )(info, *own, *come, jnp.asarray(coulomb_kernel()), consts[4], consts[5])


def inverse_kernel(info, *refs):
    pieces, own, come, last, lane_inv, field = refs[:16], *refs[16:21]
    s_buf, spec, wide, f_buf, s_sem, in_sem, out_sem = refs[21:]
    core, place = info[0], info[1]
    loads = []
    for part in range(4):
        rows = pl.ds(part * SLAB, SLAB)
        loads.append(
            [
                pltpu.make_async_copy(
                    ref.at[:, :, :, rows], spec.at[part, :, half], in_sem.at[part, side]
                )
                for side, (ref, half) in enumerate(((own, core), (come, 1 - core)))
            ]
        )
    sources = []
    for distance in range(8):
        at = lax.rem(place + 8 - distance, 8)
        for i in range(2):
            sources.append(
                pltpu.make_async_copy(
                    pieces[2 * distance + i], s_buf.at[at // 4, at % 4, i], s_sem.at[distance, i]
                )
            )
    for copy in loads[0] + sources:
        copy.start()
    for copies in loads[1:]:
        for copy in copies:
            copy.start()

    def stores(part):
        return [
            pltpu.make_async_copy(
                f_buf.at[part, p], field.at[pl.ds(4 * part + 2 * bit, 2)], out_sem.at[part, p]
            )
            for p, bit in enumerate((core, 1 - core))
        ]

    for part in range(4):
        for copy in loads[part]:
            copy.wait()
        if part == 0:
            for copy in sources:
                copy.wait()

        for h in range(2):
            for chunk in range(PLANES // CHUNK):
                half, ks = chunk // 3, pl.ds(chunk % 3 * CHUNK, CHUNK)
                p = spec[part, h, half, ks, 0].reshape(CHUNK * SLAB, N)
                q = spec[part, h, half, ks, 1].reshape(CHUNK * SLAB, N)
                out = dot(jnp.concatenate([p, q], axis=1), lane_inv[...])
                base = chunk * CHUNK
                top = min(base + CHUNK, KEPT)
                wide3 = wide.reshape(N, LAST_PITCH, N)
                wide3[pl.ds(base, top - base), 0:SLAB] = out[: (top - base) * SLAB, :N].reshape(top - base, SLAB, N)
                lo, hi = max(base, 1), min(base + CHUNK, HALF)
                wide3[pl.ds(HALF + lo, hi - lo), 0:SLAB] = out[
                    (lo - base) * SLAB : (hi - base) * SLAB, N:
                ].reshape(hi - lo, SLAB, N)
            for j in range(0, SLAB, 2):
                half_spec = jnp.concatenate(
                    [wide[pl.ds(m, N, stride=LAST_PITCH)].astype(BF16) for m in (j, j + 1)], axis=1
                )
                out = dot(last[...], half_spec)
                for m in (j, j + 1):
                    term = out[:, (m - j) * N : (m - j + 1) * N] * s_buf[
                        h, part, m // 8, m % 8
                    ].astype(F32)
                    at = (part, m // 8, m // 4 % 2, m % 4)
                    if h == 1:
                        term = f_buf[at].astype(F32) + term
                    f_buf[at] = term.astype(BF16)
        for copy in stores(part):
            copy.start()
    for part in range(4):
        for copy in stores(part):
            copy.wait()


def inverse(info, pieces, own, come, consts):
    return pl.pallas_call(
        inverse_kernel,
        out_shape=jax.ShapeDtypeStruct((16, 4, N, N), BF16),
        in_specs=[SMEM] + [HBM] * 18 + [VMEM] * 2,
        out_specs=HBM,
        scratch_shapes=[
            pltpu.VMEM((2, 4, 2, SLAB // 2, N, N), BF16),
            pltpu.VMEM((4, 2, 2, SHARE, 2, SLAB, N), BF16),
            pltpu.VMEM((LAST_PITCH * N, N), F32),
            pltpu.VMEM((4, 2, 2, 4, N, N), BF16),
            pltpu.SemaphoreType.DMA((8, 2)),
            pltpu.SemaphoreType.DMA((4, 2)),
            pltpu.SemaphoreType.DMA((4, 2)),
        ],
        compiler_params=pltpu.CompilerParams(vmem_limit_bytes=16 * MIB),
        cost_estimate=pl.CostEstimate(
            flops=2 * 14000 * 256 * 256, bytes_accessed=11 << 20, transcendentals=0
        ),
        name="inverse",
    )(info, *pieces, own, come, consts[1], consts[3])


def along_z(value, by):
    return lax.ppermute(value, ("h", "l"), [(i, (i + by) % 8) for i in range(8)])


def swap_core(value):
    return lax.ppermute(value, "c", [(0, 1), (1, 0)])


TRIPS = [
    ((4 * h + l) * 2 + bit, (l + (2, 6)[bit]) % 8 * 2 + h)
    for h in range(2)
    for l in range(4)
    for bit in range(2)
]


def to_work(value):
    return lax.ppermute(value, ("h", "l", "c"), TRIPS)


def to_owner(value):
    return lax.ppermute(value, ("h", "l", "c"), [(b, a) for a, b in TRIPS])


def over_plane(value):
    return lax.all_to_all(value, ("y", "x"), 0, 0, tiled=True)


def on_device(source_bands, target_bands):
    core = lax.axis_index("c").astype(jnp.int32)
    place = (lax.axis_index("h") * 4 + lax.axis_index("l")).astype(jnp.int32)
    consts = [jnp.asarray(t) for t in tables()]

    planes = source_bands[0].reshape(2, 2, 4, N, N)
    stay = lax.dynamic_index_in_dim(planes, core, 1, keepdims=False).reshape(8, N, N)
    other = lax.dynamic_index_in_dim(planes, 1 - core, 1, keepdims=False).reshape(8, N, N)
    other = swap_core(other)

    target, other = lax.optimization_barrier((target_bands[0], other))
    target = to_work(target)

    at = {0: (stay, other)}
    first = along_z(stay, 1), along_z(stay, -1)
    target = lax.optimization_barrier((target, *first))[0]
    t_all = over_plane(jnp.broadcast_to(target[None], (16, 4, N, N)))

    at[1] = (first[0], along_z(other, 1))
    at[7] = (first[1], along_z(other, -1))
    for k in range(2, 4):
        up, down = at[k - 1], at[9 - k]
        at[k] = tuple(along_z(piece, 1) for piece in up)
        at[8 - k] = tuple(along_z(piece, -1) for piece in down)

    own, come = [], []
    for distances in STEPS:
        if 4 in distances:
            up, down, own[0] = lax.optimization_barrier((at[3][0], at[5][1], own[0]))
            last = (along_z(up, 1), along_z(down, -1))
            *at[4], own[1] = lax.optimization_barrier((*last, own[1]))
        info = jnp.stack([core] + [(place + 8 - d) % 4 for d in distances])
        mine, give = forward(info, [p for d in distances for p in at[d]], t_all, consts)
        own.append(mine)
        come.append(swap_core(give))

    info = jnp.stack([core, place])
    mine, give = middle(info, own, come, consts)
    field = inverse(info, [p for d in range(8) for p in at[d]], mine, swap_core(give), consts)
    field = jnp.sum(over_plane(field).astype(F32), axis=0).astype(BF16)
    return to_owner(field).astype(F32)[None]


def solution(mesh):
    fine = Mesh(mesh.devices.reshape(4, 4, 2, 4, 2), ("y", "x", "h", "l", "c"))
    src, tgt = ("y", "x", "h"), ("l", "c")
    return jax.shard_map(
        on_device,
        mesh=fine,
        in_specs=(P(src, tgt, None, None), P(tgt, src, None, None)),
        out_specs=P(tgt, src, None, None),
        check_vma=False,
    )
```

time: 665 us -> 138 us (0.21); the launches traced: 656 us -> 136 us
  waiting for transfers between devices: 426 us -> 37.2 us
  matrix products: 198 us -> 0 us
  starting transfers between devices: 0.08 us -> 38.4 us
  blocking collectives: 0 us -> 32 us
  Pallas kernels: 0 us -> 22.7 us
  between operations: 13.6 us -> 0.21 us
  other arithmetic: 8.76 us -> 1.41 us
    reduce_scatter x1 -> x0, waiting for transfers between devices: 256 us -> none  [on_device(): lax.psum_scatter(band_term.astype(jnp.bfloat16), 'src', scatter_dimension...]
    dot_general x20 -> x0, matrix products: 198 us -> none  [contract(): jnp.einsum(pattern, operand, table, preferred_element_type=jnp.float32)]
    all_gather x2 -> x0, waiting for transfers between devices: 169 us -> none  [the longest x1 115 us: on_device(): target_whole = lax.all_gather(target_bands, 'src', axis=1, tiled=True)[0]]
    ppermute x0 -> x21, waiting for transfers between devices: none -> 37.2 us  [the longest x14 25.8 us: along_z(): lax.ppermute(value, ('h', 'l'), [(i, (i + by) % 8) for i in range(8)])]
    all_to_all x0 -> x1, blocking collectives: none -> 32 us  [over_plane(): return lax.all_to_all(value, ('y', 'x'), 0, 0, tiled=True)]
    ppermute x0 -> x21, starting transfers between devices: none -> 31.2 us  [the longest x14 23.7 us: along_z(): lax.ppermute(value, ('h', 'l'), [(i, (i + by) % 8) for i in range(8)])]
    pallas_call x0 -> x5, Pallas kernels: none -> 22.7 us  [the longest x3 9.52 us: forward(): pl.pallas_call(functools.partial(forward_kernel, count), out_shape=(out,...]
    all_to_all x0 -> x1, starting transfers between devices: none -> 7.17 us  [over_plane(): return lax.all_to_all(value, ('y', 'x'), 0, 0, tiled=True)]
  transfers between devices with their start and end apart: 3 -> 22, of which waited for: 3 -> 10; matrix products, arithmetic and copies ran while one was open for 0% -> 0% of each run, Pallas kernels for 0% -> 7%
where the time goes in v1:
time: 138 us; the launch traced here: 136 us
  starting transfers between devices  38.4 us (28%)
  waiting for transfers between devices  37.2 us (27%)
  blocking collectives  32 us (23%)
  Pallas kernels  22.7 us (16%)
  local copies, waits for them, and re-layouts  3.73 us (3%)
  other arithmetic  1.41 us (1%)
    all_to_all x1, blocking collectives, over_plane(): return lax.all_to_all(value, ('y', 'x'), 0, 0, tiled=True)  32 us
    ppermute x14, waiting for transfers between devices, along_z(): lax.ppermute(value, ('h', 'l'), [(i, (i + by) % 8) for i in range(8)])  25.8 us
    ppermute x14, starting transfers between devices, along_z(): lax.ppermute(value, ('h', 'l'), [(i, (i + by) % 8) for i in range(8)])  23.7 us
    pallas_call x3, Pallas kernels, forward(): pl.pallas_call(functools.partial(forward_kernel, count), out_shape=(out,...  9.52 us
    pallas_call x1, Pallas kernels, inverse(): pl.pallas_call(inverse_kernel, out_shape=jax.ShapeDtypeStruct((16, 4, N,...  7.32 us
    all_to_all x1, starting transfers between devices, over_plane(): return lax.all_to_all(value, ('y', 'x'), 0, 0, tiled=True)  7.17 us
    ppermute x5, waiting for transfers between devices, swap_core(): return lax.ppermute(value, 'c', [(0, 1), (1, 0)])  6.63 us
    pallas_call x1, Pallas kernels, middle(): pl.pallas_call(middle_kernel, out_shape=(out, out), in_specs=[SMEM] + [HB...  5.88 us
  transfers between devices with their start and end apart: 22, of which 10 were waited for; matrix products, arithmetic and copies ran while one was open for 0% of the time, Pallas kernels for 7%

profile of v1, /device:TPU:32, one launch (start us, length us, event | category | flops | bytes accessed | tf_op | source)
XLA Modules:
  0.0 135.6 jit_solution(14284779898320088698)
XLA Ops:
  0.0 1.1 constant_dynamic-slice_fusion
  1.1 0.1 collective-permute-start
  1.2 1.9 %collective-permute-start.10 = (bf16[8,128,128]{2,1,0:T(8,128)(2,1)S(1)}, bf16[8,128,128]{2,1,0:T(8,128)(2,1)S(1)}, u32[]{:S(2)}, u32[]{:S(2)}) collective-permute-start(bf16[8,128,128]{2,1,0:T(8,128)(2,1)S(1)} %bitcast.21), channel_id=1, source_target_pairs={{0,14},{2,0},{4,2},{6,4},{8,6},{10,8},{12,10},{14,12},{1,15},{3,1}... | collective-permute-start | bytes 786440 | tf_op jit(solution)/shard_map/ppermute | solution.py:326
  3.1 0.2 collective-permute-start.1
  3.3 4.5 %collective-permute-start.11 = (bf16[4,128,128]{2,1,0:T(8,128)(2,1)}, bf16[4,128,128]{2,1,0:T(8,128)(2,1)S(1)}, u32[]{:S(2)}, u32[]{:S(2)}) collective-permute-start(bf16[4,128,128]{2,1,0:T(8,128)(2,1)} %bitcast.27), channel_id=1, source_target_pairs={{0,4},{1,12},{2,6},{3,14},{4,8},{5,0},{6,10},{7,2},{8,5},{9,13},{1... | collective-permute-start | bytes 393224 | tf_op jit(solution)/shard_map/ppermute | solution.py:342
  7.8 2.4 %collective-permute-done.10.refs_4_.refs_14_ = bf16[8,128,128]{2,1,0:T(8,128)(2,1)S(1)} collective-permute-done((bf16[8,128,128]{2,1,0:T(8,128)(2,1)S(1)}, bf16[8,128,128]{2,1,0:T(8,128)(2,1)S(1)}, u32[]{:S(2)}, u32[]{:S(2)}) %collective-permute-start.10) | collective-permute-done | bytes 262176 | tf_op jit(solution)/shard_map/ppermute | solution.py:326
  10.2 3.6 %collective-permute-done.1.refs_2_ = bf16[8,128,128]{2,1,0:T(8,128)(2,1)S(1)} collective-permute-done((bf16[8,128,128]{2,1,0:T(8,128)(2,1)S(1)}, bf16[8,128,128]{2,1,0:T(8,128)(2,1)S(1)}, u32[]{:S(2)}, u32[]{:S(2)}) %collective-permute-start.1) | collective-permute-done | bytes 262176 | tf_op jit(solution)/shard_map/ppermute | solution.py:326
  13.8 1.9 %broadcast_in_dim.12 = bf16[16,4,128,128]{3,2,1,0:T(8,128)(2,1)} broadcast(bf16[4,128,128]{2,1,0:T(8,128)(2,1)S(1)} %collective-permute-done.11), dimensions={1,2,3} | broadcast | bytes 2228224 | tf_op jit(solution)/shard_map/broadcast_in_dim | solution.py:369
  15.7 7.2 %all-to-all-start = ((bf16[16,4,128,128]{3,2,1,0:T(8,128)(2,1)}), bf16[16,4,128,128]{3,2,1,0:T(8,128)(2,1)S(1)}, u32[]{:S(2)}, u32[]{:S(2)}) async-start(bf16[16,4,128,128]{3,2,1,0:T(8,128)(2,1)} %broadcast_in_dim.12), calls=%async_computation | async-start | bytes 4194304 | tf_op jit(solution)/shard_map/all_to_all | solution.py:350
  22.9 5.2 %collective-permute-start.7 = (bf16[8,128,128]{2,1,0:T(8,128)(2,1)S(1)}, bf16[8,128,128]{2,1,0:T(8,128)(2,1)S(1)}, u32[]{:S(2)}, u32[]{:S(2)}) collective-permute-start(bf16[8,128,128]{2,1,0:T(8,128)(2,1)S(1)} %collective-permute-done.refs_1_), channel_id=1, source_target_pairs={{0,14},{2,0},{4,2},{6,4},{8,6},{10,8},{12,10},{14,12},{1,15},{3,1}... | collective-permute-start | bytes 786440 | tf_op jit(solution)/shard_map/ppermute | solution.py:326
  28.1 5.6 %collective-permute-done.7.refs_5_.refs_15_ = bf16[8,128,128]{2,1,0:T(8,128)(2,1)S(1)} collective-permute-done((bf16[8,128,128]{2,1,0:T(8,128)(2,1)S(1)}, bf16[8,128,128]{2,1,0:T(8,128)(2,1)S(1)}, u32[]{:S(2)}, u32[]{:S(2)}) %collective-permute-start.7) | collective-permute-done | bytes 262176 | tf_op jit(solution)/shard_map/ppermute | solution.py:326
  33.7 2.5 %collective-permute-start.8 = (bf16[8,128,128]{2,1,0:T(8,128)(2,1)S(1)}, bf16[8,128,128]{2,1,0:T(8,128)(2,1)}, u32[]{:S(2)}, u32[]{:S(2)}) collective-permute-start(bf16[8,128,128]{2,1,0:T(8,128)(2,1)S(1)} %collective-permute-done.7.refs_5_.refs_15_), channel_id=1, source_target_pairs={{0,14},{2,0},{4,2},{6,4},{8,6},{10,8},{12,10},{14,12},{1,15},{3,1}... | collective-permute-start | bytes 786440 | tf_op jit(solution)/shard_map/ppermute | solution.py:326
  36.2 1.7 %collective-permute-start.14 = (bf16[8,128,128]{2,1,0:T(8,128)(2,1)S(1)}, bf16[8,128,128]{2,1,0:T(8,128)(2,1)}, u32[]{:S(2)}, u32[]{:S(2)}) collective-permute-start(bf16[8,128,128]{2,1,0:T(8,128)(2,1)S(1)} %collective-permute-done.10.refs_4_.refs_14_), channel_id=1, source_target_pairs={{0,14},{2,0},{4,2},{6,4},{8,6},{10,8},{12,10},{14,12},{1,15},{3,1}... | collective-permute-start | bytes 786440 | tf_op jit(solution)/shard_map/ppermute | solution.py:326
  37.9 0.3 collective-permute-start.4
  38.2 4.8 %collective-permute-done.3.refs_0_.refs_4_ = bf16[8,128,128]{2,1,0:T(8,128)(2,1)} collective-permute-done((bf16[8,128,128]{2,1,0:T(8,128)(2,1)S(1)}, bf16[8,128,128]{2,1,0:T(8,128)(2,1)}, u32[]{:S(2)}, u32[]{:S(2)}) %collective-permute-start.3) | collective-permute-done | bytes 262176 | tf_op jit(solution)/shard_map/ppermute | solution.py:326
  43.1 2.5 %collective-permute-start.9 = (bf16[8,128,128]{2,1,0:T(8,128)(2,1)}, bf16[8,128,128]{2,1,0:T(8,128)(2,1)}, u32[]{:S(2)}, u32[]{:S(2)}) collective-permute-start(bf16[8,128,128]{2,1,0:T(8,128)(2,1)} %collective-permute-done.8.refs_3_.refs_13_), channel_id=1, source_target_pairs={{0,14},{2,0},{4,2},{6,4},{8,6},{10,8},{12,10},{14,12},{1,15},{3,1}... | collective-permute-start | bytes 786440 | tf_op jit(solution)/shard_map/ppermute | solution.py:326
  45.5 0.1 pad_add_fusion.1.info
  45.6 3.0 %collective-permute-done.14.refs_2_.refs_12_ = bf16[8,128,128]{2,1,0:T(8,128)(2,1)} collective-permute-done((bf16[8,128,128]{2,1,0:T(8,128)(2,1)S(1)}, bf16[8,128,128]{2,1,0:T(8,128)(2,1)}, u32[]{:S(2)}, u32[]{:S(2)}) %collective-permute-start.14) | collective-permute-done | bytes 262176 | tf_op jit(solution)/shard_map/ppermute | solution.py:326
  48.6 2.6 %collective-permute-start.15 = (bf16[8,128,128]{2,1,0:T(8,128)(2,1)}, bf16[8,128,128]{2,1,0:T(8,128)(2,1)}, u32[]{:S(2)}, u32[]{:S(2)}) collective-permute-start(bf16[8,128,128]{2,1,0:T(8,128)(2,1)} %collective-permute-done.14.refs_2_.refs_12_), channel_id=1, source_target_pairs={{0,14},{2,0},{4,2},{6,4},{8,6},{10,8},{12,10},{14,12},{1,15},{3,1}... | collective-permute-start | bytes 786440 | tf_op jit(solution)/shard_map/ppermute | solution.py:326
  51.2 0.0 copy-start.1
  51.2 0.7 copy-done.1
  52.0 3.3 %forward.3 = (bf16[3,33,2,16,128]{4,3,2,1,0:T(8,128)(2,1)S(1)}, bf16[3,33,2,16,128]{4,3,2,1,0:T(8,128)(2,1)S(1)}) custom-call(s32[4]{0:T(128)S(1)} %pad_add_fusion.1.info, bf16[8,128,128]{2,1,0:T(8,128)(2,1)S(1)} %bitcast.23, bf16[8,128,128]{2,1,0:T(8,128)(2,1)S(1)} %collective-permute-done.refs_1_, bf16[8,128,128]{2,1,0:T(8,128)(2,1)S(1)} %collective-permute-done.1.refs_2_, ...), custom_call_target="tpu_custom_call" | custom-call | flops 688128000 | bytes 6291456 | tf_op jit(solution)/shard_map/forward/pallas_call | solution.py:120
  55.3 5.7 %collective-permute-start.12 = (bf16[8,128,128]{2,1,0:T(8,128)(2,1)}, bf16[8,128,128]{2,1,0:T(8,128)(2,1)S(1)}, u32[]{:S(2)}, u32[]{:S(2)}) collective-permute-start(bf16[8,128,128]{2,1,0:T(8,128)(2,1)} %collective-permute-done.5.refs_0_.refs_6_), channel_id=1, source_target_pairs={{0,2},{2,4},{4,6},{6,8},{8,10},{10,12},{12,14},{14,0},{1,3},{3,5},... | collective-permute-start | bytes 786440 | tf_op jit(solution)/shard_map/ppermute | solution.py:326
  60.9 1.1 collective-permute-start.13
  62.0 0.1 pad_add_fusion.2.info
  62.1 0.1 pad_add_fusion.3.info
  62.2 0.0 collective-permute-start.16
  62.3 2.7 %forward.4 = (bf16[2,33,2,16,128]{4,3,2,1,0:T(8,128)(2,1)S(1)}, bf16[2,33,2,16,128]{4,3,2,1,0:T(8,128)(2,1)S(1)}) custom-call(s32[3]{0:T(128)S(1)} %pad_add_fusion.2.info, bf16[8,128,128]{2,1,0:T(8,128)(2,1)} %collective-permute-done.3.refs_0_.refs_4_, bf16[8,128,128]{2,1,0:T(8,128)(2,1)} %collective-permute-done.4.refs_1_.refs_5_, ...), custom_call_target="tpu_custom_call" | custom-call | flops 458752000 | bytes 4194304 | tf_op jit(solution)/shard_map/forward/pallas_call | solution.py:120
  65.0 0.0 copy-start.5
  65.0 0.0 copy-start.6
  65.0 0.0 copy-start.7
  65.0 1.5 %collective-permute-done.12.refs_4_.refs_8_ = bf16[8,128,128]{2,1,0:T(8,128)(2,1)S(1)} collective-permute-done((bf16[8,128,128]{2,1,0:T(8,128)(2,1)}, bf16[8,128,128]{2,1,0:T(8,128)(2,1)S(1)}, u32[]{:S(2)}, u32[]{:S(2)}) %collective-permute-start.12) | collective-permute-done | bytes 262176 | tf_op jit(solution)/shard_map/ppermute | solution.py:326
  66.5 4.9 %collective-permute-done.13.refs_5_.refs_9_ = bf16[8,128,128]{2,1,0:T(8,128)(2,1)S(1)} collective-permute-done((bf16[8,128,128]{2,1,0:T(8,128)(2,1)}, bf16[8,128,128]{2,1,0:T(8,128)(2,1)S(1)}, u32[]{:S(2)}, u32[]{:S(2)}) %collective-permute-start.13) | collective-permute-done | bytes 262176 | tf_op jit(solution)/shard_map/ppermute | solution.py:326
  71.4 3.5 %forward.5 = (bf16[3,33,2,16,128]{4,3,2,1,0:T(8,128)(2,1)S(1)}, bf16[3,33,2,16,128]{4,3,2,1,0:T(8,128)(2,1)S(1)}) custom-call(s32[4]{0:T(128)S(1)} %pad_add_fusion.3.info, bf16[8,128,128]{2,1,0:T(8,128)(2,1)} %collective-permute-done.5.refs_0_.refs_6_, bf16[8,128,128]{2,1,0:T(8,128)(2,1)} %collective-permute-done.6.refs_1_.refs_7_, ...), custom_call_target="tpu_custom_call" | custom-call | flops 688128000 | bytes 6291456 | tf_op jit(solution)/shard_map/forward/pallas_call | solution.py:120
  74.9 0.1 collective-permute-start.18
  75.0 0.5 collective-permute-start.17
  75.5 0.1 pad_add_fusion.info
  75.6 2.5 %collective-permute-done.17.refs_4_ = bf16[2,33,2,16,128]{4,3,2,1,0:T(8,128)(2,1)S(1)} collective-permute-done((bf16[2,33,2,16,128]{4,3,2,1,0:T(8,128)(2,1)S(1)}, bf16[2,33,2,16,128]{4,3,2,1,0:T(8,128)(2,1)S(1)}, u32[]{:S(2)}, u32[]{:S(2)}) %collective-permute-start.17) | collective-permute-done | bytes 540704 | tf_op jit(solution)/shard_map/ppermute | solution.py:330
  78.1 0.0 copy-start.3
  78.2 5.9 %middle.1 = (bf16[2,33,2,64,128]{4,3,2,1,0:T(8,128)(2,1)S(1)}, bf16[2,33,2,64,128]{4,3,2,1,0:T(8,128)(2,1)S(1)}) custom-call(s32[2]{0:T(128)S(1)} %pad_add_fusion.info, bf16[3,33,2,16,128]{4,3,2,1,0:T(8,128)(2,1)S(1)} %get-tuple-element.31.refs_0_, bf16[2,33,2,16,128]{4,3,2,1,0:T(8,128)(2,1)S(1)} %get-tuple-element.32.refs_1_, ...), custom_call_target="tpu_custom_call" | custom-call | flops 2228224000 | bytes 11534336 | tf_op jit(solution)/shard_map/middle/pallas_call | solution.py:202
  84.0 0.2 collective-permute-start.19
  84.3 4.1 %collective-permute-done.19.refs_17_ = bf16[2,33,2,64,128]{4,3,2,1,0:T(8,128)(2,1)S(1)} collective-permute-done((bf16[2,33,2,64,128]{4,3,2,1,0:T(8,128)(2,1)S(1)}, bf16[2,33,2,64,128]{4,3,2,1,0:T(8,128)(2,1)S(1)}, u32[]{:S(2)}, u32[]{:S(2)}) %collective-permute-start.19) | collective-permute-done | bytes 2162720 | tf_op jit(solution)/shard_map/ppermute | solution.py:330
  88.4 7.3 %inverse.1 = bf16[16,4,128,128]{3,2,1,0:T(8,128)(2,1)S(1)} custom-call(s32[2]{0:T(128)S(1)} %pad_add_fusion.info, bf16[8,128,128]{2,1,0:T(8,128)(2,1)S(1)} %bitcast.24, bf16[8,128,128]{2,1,0:T(8,128)(2,1)S(1)} %collective-permute-done.refs_1_, bf16[8,128,128]{2,1,0:T(8,128)(2,1)S(1)} %collective-permute-done.1.refs_2_, ...), custom_call_target="tpu_custom_call" | custom-call | flops 1835008000 | bytes 11534336 | tf_op jit(solution)/shard_map/inverse/pallas_call | solution.py:303
  95.7 32.0 %all_to_all.10 = bf16[16,4,128,128]{3,2,1,0:T(8,128)(2,1)S(1)} all-to-all(bf16[16,4,128,128]{3,2,1,0:T(8,128)(2,1)S(1)} %inverse.1), channel_id=1, replica_groups=mesh['y'=4,'x'=4,'h'=2,'l'=4,'c'=2] {'y','x'}, dimensions={0} | all-to-all | bytes 4194304 | tf_op jit(solution)/shard_map/all_to_all | solution.py:350
  127.7 0.4 reduce_sum.12
  128.1 2.0 %collective-permute-start.20 = (bf16[4,128,128]{2,1,0:T(8,128)(2,1)S(1)}, bf16[4,128,128]{2,1,0:T(8,128)(2,1)S(1)}, u32[]{:S(2)}, u32[]{:S(2)}) collective-permute-start(bf16[4,128,128]{2,1,0:T(8,128)(2,1)S(1)} %reduce_sum.12), channel_id=1, source_target_pairs={{4,0},{12,1},{6,2},{14,3},{8,4},{0,5},{10,6},{2,7},{5,8},{13,9},{7... | collective-permute-start | bytes 393224 | tf_op jit(solution)/shard_map/ppermute | solution.py:346
  130.2 4.7 %collective-permute-done.20 = bf16[4,128,128]{2,1,0:T(8,128)(2,1)S(1)} collective-permute-done((bf16[4,128,128]{2,1,0:T(8,128)(2,1)S(1)}, bf16[4,128,128]{2,1,0:T(8,128)(2,1)S(1)}, u32[]{:S(2)}, u32[]{:S(2)}) %collective-permute-start.20) | collective-permute-done | bytes 131104 | tf_op jit(solution)/shard_map/ppermute | solution.py:346
  134.9 0.7 bitcast_convert_fusion
  (26 shorter events, 0.1 us)
Async XLA Ops:
  1.1 2.2 %collective-permute-start = (bf16[8,128,128]{2,1,0:T(8,128)(2,1)S(1)}, bf16[8,128,128]{2,1,0:T(8,128)(2,1)S(1)}, u32[]{:S(2)}, u32[]{:S(2)}) collective-permute-start(bf16[8,128,128]{2,1,0:T(8,128)(2,1)S(1)} %bitcast.26), channel_id=1, source_target_pairs={{0,1},{1,0},{2,3},{3,2},{4,5},{5,4},{6,7},{7,6},{8,9},{9,8},{10,11... | collective-permute-start | bytes 786440 | tf_op jit(solution)/shard_map/ppermute | solution.py:330
  1.2 9.0 %collective-permute-start.10 = (bf16[8,128,128]{2,1,0:T(8,128)(2,1)S(1)}, bf16[8,128,128]{2,1,0:T(8,128)(2,1)S(1)}, u32[]{:S(2)}, u32[]{:S(2)}) collective-permute-start(bf16[8,128,128]{2,1,0:T(8,128)(2,1)S(1)} %bitcast.21), channel_id=1, source_target_pairs={{0,14},{2,0},{4,2},{6,4},{8,6},{10,8},{12,10},{14,12},{1,15},{3,1}... | collective-permute-start | bytes 786440 | tf_op jit(solution)/shard_map/ppermute | solution.py:326
  3.1 10.7 %collective-permute-start.1 = (bf16[8,128,128]{2,1,0:T(8,128)(2,1)S(1)}, bf16[8,128,128]{2,1,0:T(8,128)(2,1)S(1)}, u32[]{:S(2)}, u32[]{:S(2)}) collective-permute-start(bf16[8,128,128]{2,1,0:T(8,128)(2,1)S(1)} %bitcast.22), channel_id=1, source_target_pairs={{0,2},{2,4},{4,6},{6,8},{8,10},{10,12},{12,14},{14,0},{1,3},{3,5},... | collective-permute-start | bytes 786440 | tf_op jit(solution)/shard_map/ppermute | solution.py:326
  3.3 10.6 %collective-permute-start.11 = (bf16[4,128,128]{2,1,0:T(8,128)(2,1)}, bf16[4,128,128]{2,1,0:T(8,128)(2,1)S(1)}, u32[]{:S(2)}, u32[]{:S(2)}) collective-permute-start(bf16[4,128,128]{2,1,0:T(8,128)(2,1)} %bitcast.27), channel_id=1, source_target_pairs={{0,4},{1,12},{2,6},{3,14},{4,8},{5,0},{6,10},{7,2},{8,5},{9,13},{1... | collective-permute-start | bytes 393224 | tf_op jit(solution)/shard_map/ppermute | solution.py:342
  15.7 35.5 %copy-start = (bf16[256,256]{1,0:T(8,128)(2,1)S(1)}, bf16[256,256]{1,0:T(8,128)(2,1)}, u32[]{:S(2)}) copy-start(bf16[256,256]{1,0:T(8,128)(2,1)} %constant.105.clone.refs_8_.refs_6_) | copy-start | bytes 393220
  15.7 35.5 %all-to-all-start = ((bf16[16,4,128,128]{3,2,1,0:T(8,128)(2,1)}), bf16[16,4,128,128]{3,2,1,0:T(8,128)(2,1)S(1)}, u32[]{:S(2)}, u32[]{:S(2)}) async-start(bf16[16,4,128,128]{3,2,1,0:T(8,128)(2,1)} %broadcast_in_dim.12), calls=%async_computation | async-start | bytes 4194304 | tf_op jit(solution)/shard_map/all_to_all | solution.py:350
  22.9 10.8 %collective-permute-start.7 = (bf16[8,128,128]{2,1,0:T(8,128)(2,1)S(1)}, bf16[8,128,128]{2,1,0:T(8,128)(2,1)S(1)}, u32[]{:S(2)}, u32[]{:S(2)}) collective-permute-start(bf16[8,128,128]{2,1,0:T(8,128)(2,1)S(1)} %collective-permute-done.refs_1_), channel_id=1, source_target_pairs={{0,14},{2,0},{4,2},{6,4},{8,6},{10,8},{12,10},{14,12},{1,15},{3,1}... | collective-permute-start | bytes 786440 | tf_op jit(solution)/shard_map/ppermute | solution.py:326
  28.1 9.8 %collective-permute-start.2 = (bf16[8,128,128]{2,1,0:T(8,128)(2,1)S(1)}, bf16[8,128,128]{2,1,0:T(8,128)(2,1)}, u32[]{:S(2)}, u32[]{:S(2)}) collective-permute-start(bf16[8,128,128]{2,1,0:T(8,128)(2,1)S(1)} %collective-permute-done.refs_1_), channel_id=1, source_target_pairs={{0,2},{2,4},{4,6},{6,8},{8,10},{10,12},{12,14},{14,0},{1,3},{3,5},... | collective-permute-start | bytes 786440 | tf_op jit(solution)/shard_map/ppermute | solution.py:326
  28.1 14.9 %collective-permute-start.3 = (bf16[8,128,128]{2,1,0:T(8,128)(2,1)S(1)}, bf16[8,128,128]{2,1,0:T(8,128)(2,1)}, u32[]{:S(2)}, u32[]{:S(2)}) collective-permute-start(bf16[8,128,128]{2,1,0:T(8,128)(2,1)S(1)} %collective-permute-done.1.refs_2_), channel_id=1, source_target_pairs={{0,2},{2,4},{4,6},{6,8},{8,10},{10,12},{12,14},{14,0},{1,3},{3,5},... | collective-permute-start | bytes 786440 | tf_op jit(solution)/shard_map/ppermute | solution.py:326
  33.7 9.3 %collective-permute-start.8 = (bf16[8,128,128]{2,1,0:T(8,128)(2,1)S(1)}, bf16[8,128,128]{2,1,0:T(8,128)(2,1)}, u32[]{:S(2)}, u32[]{:S(2)}) collective-permute-start(bf16[8,128,128]{2,1,0:T(8,128)(2,1)S(1)} %collective-permute-done.7.refs_5_.refs_15_), channel_id=1, source_target_pairs={{0,14},{2,0},{4,2},{6,4},{8,6},{10,8},{12,10},{14,12},{1,15},{3,1}... | collective-permute-start | bytes 786440 | tf_op jit(solution)/shard_map/ppermute | solution.py:326
  36.2 12.4 %collective-permute-start.14 = (bf16[8,128,128]{2,1,0:T(8,128)(2,1)S(1)}, bf16[8,128,128]{2,1,0:T(8,128)(2,1)}, u32[]{:S(2)}, u32[]{:S(2)}) collective-permute-start(bf16[8,128,128]{2,1,0:T(8,128)(2,1)S(1)} %collective-permute-done.10.refs_4_.refs_14_), channel_id=1, source_target_pairs={{0,14},{2,0},{4,2},{6,4},{8,6},{10,8},{12,10},{14,12},{1,15},{3,1}... | collective-permute-start | bytes 786440 | tf_op jit(solution)/shard_map/ppermute | solution.py:326
  37.9 13.2 %collective-permute-start.4 = (bf16[8,128,128]{2,1,0:T(8,128)(2,1)}, bf16[8,128,128]{2,1,0:T(8,128)(2,1)}, u32[]{:S(2)}, u32[]{:S(2)}) collective-permute-start(bf16[8,128,128]{2,1,0:T(8,128)(2,1)} %collective-permute-done.2.refs_3_), channel_id=1, source_target_pairs={{0,2},{2,4},{4,6},{6,8},{8,10},{10,12},{12,14},{14,0},{1,3},{3,5},... | collective-permute-start | bytes 786440 | tf_op jit(solution)/shard_map/ppermute | solution.py:326
  43.0 12.2 %collective-permute-start.5 = (bf16[8,128,128]{2,1,0:T(8,128)(2,1)}, bf16[8,128,128]{2,1,0:T(8,128)(2,1)}, u32[]{:S(2)}, u32[]{:S(2)}) collective-permute-start(bf16[8,128,128]{2,1,0:T(8,128)(2,1)} %collective-permute-done.3.refs_0_.refs_4_), channel_id=1, source_target_pairs={{0,2},{2,4},{4,6},{6,8},{8,10},{10,12},{12,14},{14,0},{1,3},{3,5},... | collective-permute-start | bytes 786440 | tf_op jit(solution)/shard_map/ppermute | solution.py:326
  43.1 12.2 %collective-permute-start.9 = (bf16[8,128,128]{2,1,0:T(8,128)(2,1)}, bf16[8,128,128]{2,1,0:T(8,128)(2,1)}, u32[]{:S(2)}, u32[]{:S(2)}) collective-permute-start(bf16[8,128,128]{2,1,0:T(8,128)(2,1)} %collective-permute-done.8.refs_3_.refs_13_), channel_id=1, source_target_pairs={{0,14},{2,0},{4,2},{6,4},{8,6},{10,8},{12,10},{14,12},{1,15},{3,1}... | collective-permute-start | bytes 786440 | tf_op jit(solution)/shard_map/ppermute | solution.py:326
  48.6 22.8 %collective-permute-start.15 = (bf16[8,128,128]{2,1,0:T(8,128)(2,1)}, bf16[8,128,128]{2,1,0:T(8,128)(2,1)}, u32[]{:S(2)}, u32[]{:S(2)}) collective-permute-start(bf16[8,128,128]{2,1,0:T(8,128)(2,1)} %collective-permute-done.14.refs_2_.refs_12_), channel_id=1, source_target_pairs={{0,14},{2,0},{4,2},{6,4},{8,6},{10,8},{12,10},{14,12},{1,15},{3,1}... | collective-permute-start | bytes 786440 | tf_op jit(solution)/shard_map/ppermute | solution.py:326
  51.2 20.2 %collective-permute-start.6 = (bf16[8,128,128]{2,1,0:T(8,128)(2,1)}, bf16[8,128,128]{2,1,0:T(8,128)(2,1)}, u32[]{:S(2)}, u32[]{:S(2)}) collective-permute-start(bf16[8,128,128]{2,1,0:T(8,128)(2,1)} %collective-permute-done.4.refs_1_.refs_5_), channel_id=1, source_target_pairs={{0,2},{2,4},{4,6},{6,8},{8,10},{10,12},{12,14},{14,0},{1,3},{3,5},... | collective-permute-start | bytes 786440 | tf_op jit(solution)/shard_map/ppermute | solution.py:326
  51.2 0.8 copy-start.1
  52.0 10.3 %copy-start.2 = (bf16[128,128]{1,0:T(8,128)(2,1)S(1)}, bf16[128,128]{1,0:T(8,128)(2,1)}, u32[]{:S(2)}) copy-start(bf16[128,128]{1,0:T(8,128)(2,1)} %constant.103.clone.refs_7_.refs_5_) | copy-start | bytes 98308
  55.3 11.3 %collective-permute-start.12 = (bf16[8,128,128]{2,1,0:T(8,128)(2,1)}, bf16[8,128,128]{2,1,0:T(8,128)(2,1)S(1)}, u32[]{:S(2)}, u32[]{:S(2)}) collective-permute-start(bf16[8,128,128]{2,1,0:T(8,128)(2,1)} %collective-permute-done.5.refs_0_.refs_6_), channel_id=1, source_target_pairs={{0,2},{2,4},{4,6},{6,8},{8,10},{10,12},{12,14},{14,0},{1,3},{3,5},... | collective-permute-start | bytes 786440 | tf_op jit(solution)/shard_map/ppermute | solution.py:326
  60.9 10.5 %collective-permute-start.13 = (bf16[8,128,128]{2,1,0:T(8,128)(2,1)}, bf16[8,128,128]{2,1,0:T(8,128)(2,1)S(1)}, u32[]{:S(2)}, u32[]{:S(2)}) collective-permute-start(bf16[8,128,128]{2,1,0:T(8,128)(2,1)} %collective-permute-done.9.refs_3_.refs_11_), channel_id=1, source_target_pairs={{0,14},{2,0},{4,2},{6,4},{8,6},{10,8},{12,10},{14,12},{1,15},{3,1}... | collective-permute-start | bytes 786440 | tf_op jit(solution)/shard_map/ppermute | solution.py:326
  62.2 15.9 %collective-permute-start.16 = (bf16[3,33,2,16,128]{4,3,2,1,0:T(8,128)(2,1)S(1)}, bf16[3,33,2,16,128]{4,3,2,1,0:T(8,128)(2,1)S(1)}, u32[]{:S(2)}, u32[]{:S(2)}) collective-permute-start(bf16[3,33,2,16,128]{4,3,2,1,0:T(8,128)(2,1)S(1)} %get-tuple-element.34), channel_id=1, source_target_pairs={{0,1},{1,0},{2,3},{3,2},{4,5},{5,4},{6,7},{7,6},{8,9},{9,8},{10,11... | collective-permute-start | bytes 2433032 | tf_op jit(solution)/shard_map/ppermute | solution.py:330
  65.0 13.1 %copy-start.5 = (bf16[2,33,128,128]{3,2,1,0:T(8,128)(2,1)S(1)}, bf16[2,33,128,128]{3,2,1,0:T(8,128)(2,1)}, u32[]{:S(2)}) copy-start(bf16[2,33,128,128]{3,2,1,0:T(8,128)(2,1)} %constant.109.clone.refs_6_) | copy-start | bytes 6488068
  65.0 13.1 %copy-start.6 = (bf16[256,256]{1,0:T(8,128)(2,1)S(1)}, bf16[256,256]{1,0:T(8,128)(2,1)}, u32[]{:S(2)}) copy-start(bf16[256,256]{1,0:T(8,128)(2,1)} %constant.108.clone.refs_8_) | copy-start | bytes 393220
  65.0 13.1 %copy-start.7 = (bf16[256,256]{1,0:T(8,128)(2,1)S(1)}, bf16[256,256]{1,0:T(8,128)(2,1)}, u32[]{:S(2)}) copy-start(bf16[256,256]{1,0:T(8,128)(2,1)} %constant.107.clone.refs_7_) | copy-start | bytes 393220
  74.9 3.2 %collective-permute-start.18 = (bf16[3,33,2,16,128]{4,3,2,1,0:T(8,128)(2,1)S(1)}, bf16[3,33,2,16,128]{4,3,2,1,0:T(8,128)(2,1)S(1)}, u32[]{:S(2)}, u32[]{:S(2)}) collective-permute-start(bf16[3,33,2,16,128]{4,3,2,1,0:T(8,128)(2,1)S(1)} %get-tuple-element.36), channel_id=1, source_target_pairs={{0,1},{1,0},{2,3},{3,2},{4,5},{5,4},{6,7},{7,6},{8,9},{9,8},{10,11... | collective-permute-start | bytes 2433032 | tf_op jit(solution)/shard_map/ppermute | solution.py:330
  75.0 3.1 %collective-permute-start.17 = (bf16[2,33,2,16,128]{4,3,2,1,0:T(8,128)(2,1)S(1)}, bf16[2,33,2,16,128]{4,3,2,1,0:T(8,128)(2,1)S(1)}, u32[]{:S(2)}, u32[]{:S(2)}) collective-permute-start(bf16[2,33,2,16,128]{4,3,2,1,0:T(8,128)(2,1)S(1)} %get-tuple-element.35), channel_id=1, source_target_pairs={{0,1},{1,0},{2,3},{3,2},{4,5},{5,4},{6,7},{7,6},{8,9},{9,8},{10,11... | collective-permute-start | bytes 1622024 | tf_op jit(solution)/shard_map/ppermute | solution.py:330
  78.1 10.3 %copy-start.3 = (bf16[256,256]{1,0:T(8,128)(2,1)S(1)}, bf16[256,256]{1,0:T(8,128)(2,1)}, u32[]{:S(2)}) copy-start(bf16[256,256]{1,0:T(8,128)(2,1)} %constant.106.clone.refs_19_) | copy-start | bytes 393220
  78.1 10.2 %copy-start.4 = (bf16[128,128]{1,0:T(8,128)(2,1)S(1)}, bf16[128,128]{1,0:T(8,128)(2,1)}, u32[]{:S(2)}) copy-start(bf16[128,128]{1,0:T(8,128)(2,1)} %constant.104.clone.refs_18_) | copy-start | bytes 98308
  84.0 4.3 %collective-permute-start.19 = (bf16[2,33,2,64,128]{4,3,2,1,0:T(8,128)(2,1)S(1)}, bf16[2,33,2,64,128]{4,3,2,1,0:T(8,128)(2,1)S(1)}, u32[]{:S(2)}, u32[]{:S(2)}) collective-permute-start(bf16[2,33,2,64,128]{4,3,2,1,0:T(8,128)(2,1)S(1)} %get-tuple-element.38), channel_id=1, source_target_pairs={{0,1},{1,0},{2,3},{3,2},{4,5},{5,4},{6,7},{7,6},{8,9},{9,8},{10,11... | collective-permute-start | bytes 6488072 | tf_op jit(solution)/shard_map/ppermute | solution.py:330
  128.1 6.8 %collective-permute-start.20 = (bf16[4,128,128]{2,1,0:T(8,128)(2,1)S(1)}, bf16[4,128,128]{2,1,0:T(8,128)(2,1)S(1)}, u32[]{:S(2)}, u32[]{:S(2)}) collective-permute-start(bf16[4,128,128]{2,1,0:T(8,128)(2,1)S(1)} %reduce_sum.12), channel_id=1, source_target_pairs={{4,0},{12,1},{6,2},{14,3},{8,4},{0,5},{10,6},{2,7},{5,8},{13,9},{7... | collective-permute-start | bytes 393224 | tf_op jit(solution)/shard_map/ppermute | solution.py:346

commit v2 on v1

--- a/solution.py
+++ b/solution.py
@@ -261,9 +261,12 @@
     for part in range(4):
         for copy in loads[part]:
             copy.wait()
-        if part == 0:
-            for copy in sources:
-                copy.wait()
+        for h in range(2):
+            distance = lax.rem(place + 8 - (4 * h + part), 8)
+            for i in range(2):
+                pltpu.make_async_copy(
+                    pieces[i], s_buf.at[h, part, i], s_sem.at[distance, i]
+                ).wait()
 
         for h in range(2):
             for chunk in range(PLANES // CHUNK):
@@ -365,7 +368,6 @@
 
     at = {0: (stay, other)}
     first = along_z(stay, 1), along_z(stay, -1)
-    target = lax.optimization_barrier((target, *first))[0]
     t_all = over_plane(jnp.broadcast_to(target[None], (16, 4, N, N)))
 
     at[1] = (first[0], along_z(other, 1))

time: 138 us -> 136 us (0.986)
  the two profiles are of different devices: /device:TPU:32 before, /device:TPU:64 now
where the time goes in v2:
time: 136 us
  waiting for transfers between devices  40.6 us (30%)
  blocking collectives  34.9 us (26%)
  starting transfers between devices  32.5 us (24%)
  Pallas kernels  22.8 us (17%)
  local copies, waits for them, and re-layouts  3.73 us (3%)
  other arithmetic  1.41 us (1%)
    all_to_all x1, blocking collectives, over_plane(): return lax.all_to_all(value, ('y', 'x'), 0, 0, tiled=True)  34.9 us
    ppermute x14, starting transfers between devices, along_z(): lax.ppermute(value, ('h', 'l'), [(i, (i + by) % 8) for i in range(8)])  19.8 us
    ppermute x14, waiting for transfers between devices, along_z(): lax.ppermute(value, ('h', 'l'), [(i, (i + by) % 8) for i in range(8)])  18.1 us
    pallas_call x3, Pallas kernels, forward(): pl.pallas_call(functools.partial(forward_kernel, count), out_shape=(out,...  9.52 us
    ppermute x1, waiting for transfers between devices, to_owner(): return lax.ppermute(value, ('h', 'l', 'c'), [(b, a) for a, b in TRIPS])  8.47 us
    ppermute x5, waiting for transfers between devices, swap_core(): return lax.ppermute(value, 'c', [(0, 1), (1, 0)])  8.15 us
    pallas_call x1, Pallas kernels, inverse(): pl.pallas_call(inverse_kernel, out_shape=jax.ShapeDtypeStruct((16, 4, N,...  7.38 us
    all_to_all x1, starting transfers between devices, over_plane(): return lax.all_to_all(value, ('y', 'x'), 0, 0, tiled=True)  7.17 us
  transfers between devices with their start and end apart: 22, of which 12 were waited for; matrix products, arithmetic and copies ran while one was open for 0% of the time, Pallas kernels for 7%

profile of v2, /device:TPU:64, one launch (start us, length us, event | category | flops | bytes accessed | tf_op | source)
XLA Modules:
  0.0 136.0 jit_solution(12338958522735066785)
XLA Ops:
  0.0 1.1 constant_dynamic-slice_fusion
  1.1 0.1 collective-permute-start
  1.2 1.5 %collective-permute-done.refs_1_ = bf16[8,128,128]{2,1,0:T(8,128)(2,1)S(1)} collective-permute-done((bf16[8,128,128]{2,1,0:T(8,128)(2,1)S(1)}, bf16[8,128,128]{2,1,0:T(8,128)(2,1)S(1)}, u32[]{:S(2)}, u32[]{:S(2)}) %collective-permute-start) | collective-permute-done | bytes 262176 | tf_op jit(solution)/shard_map/ppermute | solution.py:333
  2.7 4.5 %collective-permute-start.11 = (bf16[4,128,128]{2,1,0:T(8,128)(2,1)}, bf16[4,128,128]{2,1,0:T(8,128)(2,1)S(1)}, u32[]{:S(2)}, u32[]{:S(2)}) collective-permute-start(bf16[4,128,128]{2,1,0:T(8,128)(2,1)} %bitcast.27), channel_id=1, source_target_pairs={{0,4},{1,12},{2,6},{3,14},{4,8},{5,0},{6,10},{7,2},{8,5},{9,13},{1... | collective-permute-start | bytes 393224 | tf_op jit(solution)/shard_map/ppermute | solution.py:345
  7.2 3.5 %collective-permute-done.11 = bf16[4,128,128]{2,1,0:T(8,128)(2,1)S(1)} collective-permute-done((bf16[4,128,128]{2,1,0:T(8,128)(2,1)}, bf16[4,128,128]{2,1,0:T(8,128)(2,1)S(1)}, u32[]{:S(2)}, u32[]{:S(2)}) %collective-permute-start.11) | collective-permute-done | bytes 131104 | tf_op jit(solution)/shard_map/ppermute | solution.py:345
  10.7 1.9 %broadcast_in_dim.12 = bf16[16,4,128,128]{3,2,1,0:T(8,128)(2,1)} broadcast(bf16[4,128,128]{2,1,0:T(8,128)(2,1)S(1)} %collective-permute-done.11), dimensions={1,2,3} | broadcast | bytes 2228224 | tf_op jit(solution)/shard_map/broadcast_in_dim | solution.py:371
  12.6 7.2 %all-to-all-start = ((bf16[16,4,128,128]{3,2,1,0:T(8,128)(2,1)}), bf16[16,4,128,128]{3,2,1,0:T(8,128)(2,1)S(1)}, u32[]{:S(2)}, u32[]{:S(2)}) async-start(bf16[16,4,128,128]{3,2,1,0:T(8,128)(2,1)} %broadcast_in_dim.12), calls=%async_computation | async-start | bytes 4194304 | tf_op jit(solution)/shard_map/all_to_all | solution.py:353
  19.8 1.1 collective-permute-start.1
  20.8 1.0 collective-permute-start.7
  21.9 0.0 collective-permute-start.10
  21.9 3.1 %collective-permute-start.2 = (bf16[8,128,128]{2,1,0:T(8,128)(2,1)S(1)}, bf16[8,128,128]{2,1,0:T(8,128)(2,1)}, u32[]{:S(2)}, u32[]{:S(2)}) collective-permute-start(bf16[8,128,128]{2,1,0:T(8,128)(2,1)S(1)} %collective-permute-done.refs_1_), channel_id=1, source_target_pairs={{0,2},{2,4},{4,6},{6,8},{8,10},{10,12},{12,14},{14,0},{1,3},{3,5},... | collective-permute-start | bytes 786440 | tf_op jit(solution)/shard_map/ppermute | solution.py:329
  25.0 4.0 %collective-permute-done.1.refs_2_ = bf16[8,128,128]{2,1,0:T(8,128)(2,1)S(1)} collective-permute-done((bf16[8,128,128]{2,1,0:T(8,128)(2,1)S(1)}, bf16[8,128,128]{2,1,0:T(8,128)(2,1)S(1)}, u32[]{:S(2)}, u32[]{:S(2)}) %collective-permute-start.1) | collective-permute-done | bytes 262176 | tf_op jit(solution)/shard_map/ppermute | solution.py:329
  28.9 2.8 %collective-permute-start.3 = (bf16[8,128,128]{2,1,0:T(8,128)(2,1)S(1)}, bf16[8,128,128]{2,1,0:T(8,128)(2,1)}, u32[]{:S(2)}, u32[]{:S(2)}) collective-permute-start(bf16[8,128,128]{2,1,0:T(8,128)(2,1)S(1)} %collective-permute-done.1.refs_2_), channel_id=1, source_target_pairs={{0,2},{2,4},{4,6},{6,8},{8,10},{10,12},{12,14},{14,0},{1,3},{3,5},... | collective-permute-start | bytes 786440 | tf_op jit(solution)/shard_map/ppermute | solution.py:329
  31.7 0.5 collective-permute-done.7.refs_5_.refs_15_
  32.2 5.6 %collective-permute-done.10.refs_4_.refs_14_ = bf16[8,128,128]{2,1,0:T(8,128)(2,1)S(1)} collective-permute-done((bf16[8,128,128]{2,1,0:T(8,128)(2,1)S(1)}, bf16[8,128,128]{2,1,0:T(8,128)(2,1)S(1)}, u32[]{:S(2)}, u32[]{:S(2)}) %collective-permute-start.10) | collective-permute-done | bytes 262176 | tf_op jit(solution)/shard_map/ppermute | solution.py:329
  37.8 3.2 %collective-permute-start.4 = (bf16[8,128,128]{2,1,0:T(8,128)(2,1)}, bf16[8,128,128]{2,1,0:T(8,128)(2,1)}, u32[]{:S(2)}, u32[]{:S(2)}) collective-permute-start(bf16[8,128,128]{2,1,0:T(8,128)(2,1)} %collective-permute-done.2.refs_3_), channel_id=1, source_target_pairs={{0,2},{2,4},{4,6},{6,8},{8,10},{10,12},{12,14},{14,0},{1,3},{3,5},... | collective-permute-start | bytes 786440 | tf_op jit(solution)/shard_map/ppermute | solution.py:329
  41.0 3.2 %collective-permute-start.5 = (bf16[8,128,128]{2,1,0:T(8,128)(2,1)}, bf16[8,128,128]{2,1,0:T(8,128)(2,1)}, u32[]{:S(2)}, u32[]{:S(2)}) collective-permute-start(bf16[8,128,128]{2,1,0:T(8,128)(2,1)} %collective-permute-done.3.refs_0_.refs_4_), channel_id=1, source_target_pairs={{0,2},{2,4},{4,6},{6,8},{8,10},{10,12},{12,14},{14,0},{1,3},{3,5},... | collective-permute-start | bytes 786440 | tf_op jit(solution)/shard_map/ppermute | solution.py:329
  44.3 0.1 pad_add_fusion.1.info
  44.3 4.8 %collective-permute-done.14.refs_2_.refs_12_ = bf16[8,128,128]{2,1,0:T(8,128)(2,1)} collective-permute-done((bf16[8,128,128]{2,1,0:T(8,128)(2,1)S(1)}, bf16[8,128,128]{2,1,0:T(8,128)(2,1)}, u32[]{:S(2)}, u32[]{:S(2)}) %collective-permute-start.14) | collective-permute-done | bytes 262176 | tf_op jit(solution)/shard_map/ppermute | solution.py:329
  49.1 3.2 %collective-permute-start.6 = (bf16[8,128,128]{2,1,0:T(8,128)(2,1)}, bf16[8,128,128]{2,1,0:T(8,128)(2,1)}, u32[]{:S(2)}, u32[]{:S(2)}) collective-permute-start(bf16[8,128,128]{2,1,0:T(8,128)(2,1)} %collective-permute-done.4.refs_1_.refs_5_), channel_id=1, source_target_pairs={{0,2},{2,4},{4,6},{6,8},{8,10},{10,12},{12,14},{14,0},{1,3},{3,5},... | collective-permute-start | bytes 786440 | tf_op jit(solution)/shard_map/ppermute | solution.py:329
  52.4 2.3 %all-to-all-done.refs_6_.refs_4_ = bf16[16,4,128,128]{3,2,1,0:T(8,128)(2,1)S(1)} async-done(((bf16[16,4,128,128]{3,2,1,0:T(8,128)(2,1)}), bf16[16,4,128,128]{3,2,1,0:T(8,128)(2,1)S(1)}, u32[]{:S(2)}, u32[]{:S(2)}) %all-to-all-start) | async-done | bytes 2097184 | tf_op jit(solution)/shard_map/all_to_all | solution.py:353
  54.6 0.8 copy-done.1
  55.4 3.3 %forward.3 = (bf16[3,33,2,16,128]{4,3,2,1,0:T(8,128)(2,1)S(1)}, bf16[3,33,2,16,128]{4,3,2,1,0:T(8,128)(2,1)S(1)}) custom-call(s32[4]{0:T(128)S(1)} %pad_add_fusion.1.info, bf16[8,128,128]{2,1,0:T(8,128)(2,1)S(1)} %bitcast.23, bf16[8,128,128]{2,1,0:T(8,128)(2,1)S(1)} %collective-permute-done.refs_1_, bf16[8,128,128]{2,1,0:T(8,128)(2,1)S(1)} %collective-permute-done.1.refs_2_, ...), custom_call_target="tpu_custom_call" | custom-call | flops 688128000 | bytes 6291456 | tf_op jit(solution)/shard_map/forward/pallas_call | solution.py:120
  58.7 1.0 collective-permute-start.12
  59.8 1.1 collective-permute-start.13
  60.8 0.1 pad_add_fusion.2.info
  60.9 0.1 pad_add_fusion.3.info
  61.0 0.0 collective-permute-start.16
  61.0 2.7 %forward.4 = (bf16[2,33,2,16,128]{4,3,2,1,0:T(8,128)(2,1)S(1)}, bf16[2,33,2,16,128]{4,3,2,1,0:T(8,128)(2,1)S(1)}) custom-call(s32[3]{0:T(128)S(1)} %pad_add_fusion.2.info, bf16[8,128,128]{2,1,0:T(8,128)(2,1)} %collective-permute-done.3.refs_0_.refs_4_, bf16[8,128,128]{2,1,0:T(8,128)(2,1)} %collective-permute-done.4.refs_1_.refs_5_, ...), custom_call_target="tpu_custom_call" | custom-call | flops 458752000 | bytes 4194304 | tf_op jit(solution)/shard_map/forward/pallas_call | solution.py:120
  63.8 0.0 copy-start.5
  63.8 0.0 copy-start.6
  63.8 0.0 copy-start.7
  63.8 3.2 %collective-permute-done.12.refs_4_.refs_8_ = bf16[8,128,128]{2,1,0:T(8,128)(2,1)S(1)} collective-permute-done((bf16[8,128,128]{2,1,0:T(8,128)(2,1)}, bf16[8,128,128]{2,1,0:T(8,128)(2,1)S(1)}, u32[]{:S(2)}, u32[]{:S(2)}) %collective-permute-start.12) | collective-permute-done | bytes 262176 | tf_op jit(solution)/shard_map/ppermute | solution.py:329
  67.0 0.1 collective-permute-done.13.refs_5_.refs_9_
  67.1 3.5 %forward.5 = (bf16[3,33,2,16,128]{4,3,2,1,0:T(8,128)(2,1)S(1)}, bf16[3,33,2,16,128]{4,3,2,1,0:T(8,128)(2,1)S(1)}) custom-call(s32[4]{0:T(128)S(1)} %pad_add_fusion.3.info, bf16[8,128,128]{2,1,0:T(8,128)(2,1)} %collective-permute-done.5.refs_0_.refs_6_, bf16[8,128,128]{2,1,0:T(8,128)(2,1)} %collective-permute-done.6.refs_1_.refs_7_, ...), custom_call_target="tpu_custom_call" | custom-call | flops 688128000 | bytes 6291456 | tf_op jit(solution)/shard_map/forward/pallas_call | solution.py:120
  70.6 0.1 collective-permute-start.18
  70.7 0.5 collective-permute-start.17
  71.2 0.1 pad_add_fusion.info
  71.3 2.5 %collective-permute-done.17.refs_4_ = bf16[2,33,2,16,128]{4,3,2,1,0:T(8,128)(2,1)S(1)} collective-permute-done((bf16[2,33,2,16,128]{4,3,2,1,0:T(8,128)(2,1)S(1)}, bf16[2,33,2,16,128]{4,3,2,1,0:T(8,128)(2,1)S(1)}, u32[]{:S(2)}, u32[]{:S(2)}) %collective-permute-start.17) | collective-permute-done | bytes 540704 | tf_op jit(solution)/shard_map/ppermute | solution.py:333
  73.9 5.9 %middle.1 = (bf16[2,33,2,64,128]{4,3,2,1,0:T(8,128)(2,1)S(1)}, bf16[2,33,2,64,128]{4,3,2,1,0:T(8,128)(2,1)S(1)}) custom-call(s32[2]{0:T(128)S(1)} %pad_add_fusion.info, bf16[3,33,2,16,128]{4,3,2,1,0:T(8,128)(2,1)S(1)} %get-tuple-element.29.refs_0_, bf16[2,33,2,16,128]{4,3,2,1,0:T(8,128)(2,1)S(1)} %get-tuple-element.30.refs_1_, ...), custom_call_target="tpu_custom_call" | custom-call | flops 2228224000 | bytes 11534336 | tf_op jit(solution)/shard_map/middle/pallas_call | solution.py:202
  79.7 0.2 collective-permute-start.19
  80.0 4.1 %collective-permute-done.19.refs_17_ = bf16[2,33,2,64,128]{4,3,2,1,0:T(8,128)(2,1)S(1)} collective-permute-done((bf16[2,33,2,64,128]{4,3,2,1,0:T(8,128)(2,1)S(1)}, bf16[2,33,2,64,128]{4,3,2,1,0:T(8,128)(2,1)S(1)}, u32[]{:S(2)}, u32[]{:S(2)}) %collective-permute-start.19) | collective-permute-done | bytes 2162720 | tf_op jit(solution)/shard_map/ppermute | solution.py:333
  84.1 7.4 %inverse.1 = bf16[16,4,128,128]{3,2,1,0:T(8,128)(2,1)S(1)} custom-call(s32[2]{0:T(128)S(1)} %pad_add_fusion.info, bf16[8,128,128]{2,1,0:T(8,128)(2,1)S(1)} %bitcast.24, bf16[8,128,128]{2,1,0:T(8,128)(2,1)S(1)} %collective-permute-done.refs_1_, bf16[8,128,128]{2,1,0:T(8,128)(2,1)S(1)} %collective-permute-done.1.refs_2_, ...), custom_call_target="tpu_custom_call" | custom-call | flops 1835008000 | bytes 11534336 | tf_op jit(solution)/shard_map/inverse/pallas_call | solution.py:306
  91.5 34.9 %all_to_all.10 = bf16[16,4,128,128]{3,2,1,0:T(8,128)(2,1)S(1)} all-to-all(bf16[16,4,128,128]{3,2,1,0:T(8,128)(2,1)S(1)} %inverse.1), channel_id=1, replica_groups=mesh['y'=4,'x'=4,'h'=2,'l'=4,'c'=2] {'y','x'}, dimensions={0} | all-to-all | bytes 4194304 | tf_op jit(solution)/shard_map/all_to_all | solution.py:353
  126.4 0.4 reduce_sum.12
  126.7 0.1 collective-permute-start.20
  126.8 8.5 %collective-permute-done.20 = bf16[4,128,128]{2,1,0:T(8,128)(2,1)S(1)} collective-permute-done((bf16[4,128,128]{2,1,0:T(8,128)(2,1)S(1)}, bf16[4,128,128]{2,1,0:T(8,128)(2,1)S(1)}, u32[]{:S(2)}, u32[]{:S(2)}) %collective-permute-start.20) | collective-permute-done | bytes 131104 | tf_op jit(solution)/shard_map/ppermute | solution.py:349
  135.3 0.7 bitcast_convert_fusion
  (26 shorter events, 0.1 us)
Async XLA Ops:
  1.1 1.6 %collective-permute-start = (bf16[8,128,128]{2,1,0:T(8,128)(2,1)S(1)}, bf16[8,128,128]{2,1,0:T(8,128)(2,1)S(1)}, u32[]{:S(2)}, u32[]{:S(2)}) collective-permute-start(bf16[8,128,128]{2,1,0:T(8,128)(2,1)S(1)} %bitcast.26), channel_id=1, source_target_pairs={{0,1},{1,0},{2,3},{3,2},{4,5},{5,4},{6,7},{7,6},{8,9},{9,8},{10,11... | collective-permute-start | bytes 786440 | tf_op jit(solution)/shard_map/ppermute | solution.py:333
  2.7 8.0 %collective-permute-start.11 = (bf16[4,128,128]{2,1,0:T(8,128)(2,1)}, bf16[4,128,128]{2,1,0:T(8,128)(2,1)S(1)}, u32[]{:S(2)}, u32[]{:S(2)}) collective-permute-start(bf16[4,128,128]{2,1,0:T(8,128)(2,1)} %bitcast.27), channel_id=1, source_target_pairs={{0,4},{1,12},{2,6},{3,14},{4,8},{5,0},{6,10},{7,2},{8,5},{9,13},{1... | collective-permute-start | bytes 393224 | tf_op jit(solution)/shard_map/ppermute | solution.py:345
  12.6 42.0 %copy-start = (bf16[256,256]{1,0:T(8,128)(2,1)S(1)}, bf16[256,256]{1,0:T(8,128)(2,1)}, u32[]{:S(2)}) copy-start(bf16[256,256]{1,0:T(8,128)(2,1)} %constant.105.clone.refs_8_.refs_6_) | copy-start | bytes 393220
  12.6 42.0 %all-to-all-start = ((bf16[16,4,128,128]{3,2,1,0:T(8,128)(2,1)}), bf16[16,4,128,128]{3,2,1,0:T(8,128)(2,1)S(1)}, u32[]{:S(2)}, u32[]{:S(2)}) async-start(bf16[16,4,128,128]{3,2,1,0:T(8,128)(2,1)} %broadcast_in_dim.12), calls=%async_computation | async-start | bytes 4194304 | tf_op jit(solution)/shard_map/all_to_all | solution.py:353
  19.8 9.2 %collective-permute-start.1 = (bf16[8,128,128]{2,1,0:T(8,128)(2,1)S(1)}, bf16[8,128,128]{2,1,0:T(8,128)(2,1)S(1)}, u32[]{:S(2)}, u32[]{:S(2)}) collective-permute-start(bf16[8,128,128]{2,1,0:T(8,128)(2,1)S(1)} %bitcast.21), channel_id=1, source_target_pairs={{0,2},{2,4},{4,6},{6,8},{8,10},{10,12},{12,14},{14,0},{1,3},{3,5},... | collective-permute-start | bytes 786440 | tf_op jit(solution)/shard_map/ppermute | solution.py:329
  20.8 11.3 %collective-permute-start.7 = (bf16[8,128,128]{2,1,0:T(8,128)(2,1)S(1)}, bf16[8,128,128]{2,1,0:T(8,128)(2,1)S(1)}, u32[]{:S(2)}, u32[]{:S(2)}) collective-permute-start(bf16[8,128,128]{2,1,0:T(8,128)(2,1)S(1)} %collective-permute-done.refs_1_), channel_id=1, source_target_pairs={{0,14},{2,0},{4,2},{6,4},{8,6},{10,8},{12,10},{14,12},{1,15},{3,1}... | collective-permute-start | bytes 786440 | tf_op jit(solution)/shard_map/ppermute | solution.py:329
  21.9 15.9 %collective-permute-start.10 = (bf16[8,128,128]{2,1,0:T(8,128)(2,1)S(1)}, bf16[8,128,128]{2,1,0:T(8,128)(2,1)S(1)}, u32[]{:S(2)}, u32[]{:S(2)}) collective-permute-start(bf16[8,128,128]{2,1,0:T(8,128)(2,1)S(1)} %bitcast.22), channel_id=1, source_target_pairs={{0,14},{2,0},{4,2},{6,4},{8,6},{10,8},{12,10},{14,12},{1,15},{3,1}... | collective-permute-start | bytes 786440 | tf_op jit(solution)/shard_map/ppermute | solution.py:329
  21.9 15.9 %collective-permute-start.2 = (bf16[8,128,128]{2,1,0:T(8,128)(2,1)S(1)}, bf16[8,128,128]{2,1,0:T(8,128)(2,1)}, u32[]{:S(2)}, u32[]{:S(2)}) collective-permute-start(bf16[8,128,128]{2,1,0:T(8,128)(2,1)S(1)} %collective-permute-done.refs_1_), channel_id=1, source_target_pairs={{0,2},{2,4},{4,6},{6,8},{8,10},{10,12},{12,14},{14,0},{1,3},{3,5},... | collective-permute-start | bytes 786440 | tf_op jit(solution)/shard_map/ppermute | solution.py:329
  28.9 12.1 %collective-permute-start.3 = (bf16[8,128,128]{2,1,0:T(8,128)(2,1)S(1)}, bf16[8,128,128]{2,1,0:T(8,128)(2,1)}, u32[]{:S(2)}, u32[]{:S(2)}) collective-permute-start(bf16[8,128,128]{2,1,0:T(8,128)(2,1)S(1)} %collective-permute-done.1.refs_2_), channel_id=1, source_target_pairs={{0,2},{2,4},{4,6},{6,8},{8,10},{10,12},{12,14},{14,0},{1,3},{3,5},... | collective-permute-start | bytes 786440 | tf_op jit(solution)/shard_map/ppermute | solution.py:329
  32.2 12.1 %collective-permute-start.8 = (bf16[8,128,128]{2,1,0:T(8,128)(2,1)S(1)}, bf16[8,128,128]{2,1,0:T(8,128)(2,1)}, u32[]{:S(2)}, u32[]{:S(2)}) collective-permute-start(bf16[8,128,128]{2,1,0:T(8,128)(2,1)S(1)} %collective-permute-done.7.refs_5_.refs_15_), channel_id=1, source_target_pairs={{0,14},{2,0},{4,2},{6,4},{8,6},{10,8},{12,10},{14,12},{1,15},{3,1}... | collective-permute-start | bytes 786440 | tf_op jit(solution)/shard_map/ppermute | solution.py:329
  37.8 11.3 %collective-permute-start.14 = (bf16[8,128,128]{2,1,0:T(8,128)(2,1)S(1)}, bf16[8,128,128]{2,1,0:T(8,128)(2,1)}, u32[]{:S(2)}, u32[]{:S(2)}) collective-permute-start(bf16[8,128,128]{2,1,0:T(8,128)(2,1)S(1)} %collective-permute-done.10.refs_4_.refs_14_), channel_id=1, source_target_pairs={{0,14},{2,0},{4,2},{6,4},{8,6},{10,8},{12,10},{14,12},{1,15},{3,1}... | collective-permute-start | bytes 786440 | tf_op jit(solution)/shard_map/ppermute | solution.py:329
  37.8 11.3 %collective-permute-start.4 = (bf16[8,128,128]{2,1,0:T(8,128)(2,1)}, bf16[8,128,128]{2,1,0:T(8,128)(2,1)}, u32[]{:S(2)}, u32[]{:S(2)}) collective-permute-start(bf16[8,128,128]{2,1,0:T(8,128)(2,1)} %collective-permute-done.2.refs_3_), channel_id=1, source_target_pairs={{0,2},{2,4},{4,6},{6,8},{8,10},{10,12},{12,14},{14,0},{1,3},{3,5},... | collective-permute-start | bytes 786440 | tf_op jit(solution)/shard_map/ppermute | solution.py:329
  41.0 17.7 %collective-permute-start.5 = (bf16[8,128,128]{2,1,0:T(8,128)(2,1)}, bf16[8,128,128]{2,1,0:T(8,128)(2,1)}, u32[]{:S(2)}, u32[]{:S(2)}) collective-permute-start(bf16[8,128,128]{2,1,0:T(8,128)(2,1)} %collective-permute-done.3.refs_0_.refs_4_), channel_id=1, source_target_pairs={{0,2},{2,4},{4,6},{6,8},{8,10},{10,12},{12,14},{14,0},{1,3},{3,5},... | collective-permute-start | bytes 786440 | tf_op jit(solution)/shard_map/ppermute | solution.py:329
  44.3 14.4 %collective-permute-start.9 = (bf16[8,128,128]{2,1,0:T(8,128)(2,1)}, bf16[8,128,128]{2,1,0:T(8,128)(2,1)}, u32[]{:S(2)}, u32[]{:S(2)}) collective-permute-start(bf16[8,128,128]{2,1,0:T(8,128)(2,1)} %collective-permute-done.8.refs_3_.refs_13_), channel_id=1, source_target_pairs={{0,14},{2,0},{4,2},{6,4},{8,6},{10,8},{12,10},{14,12},{1,15},{3,1}... | collective-permute-start | bytes 786440 | tf_op jit(solution)/shard_map/ppermute | solution.py:329
  49.1 18.0 %collective-permute-start.15 = (bf16[8,128,128]{2,1,0:T(8,128)(2,1)}, bf16[8,128,128]{2,1,0:T(8,128)(2,1)}, u32[]{:S(2)}, u32[]{:S(2)}) collective-permute-start(bf16[8,128,128]{2,1,0:T(8,128)(2,1)} %collective-permute-done.14.refs_2_.refs_12_), channel_id=1, source_target_pairs={{0,14},{2,0},{4,2},{6,4},{8,6},{10,8},{12,10},{14,12},{1,15},{3,1}... | collective-permute-start | bytes 786440 | tf_op jit(solution)/shard_map/ppermute | solution.py:329
  49.1 18.0 %collective-permute-start.6 = (bf16[8,128,128]{2,1,0:T(8,128)(2,1)}, bf16[8,128,128]{2,1,0:T(8,128)(2,1)}, u32[]{:S(2)}, u32[]{:S(2)}) collective-permute-start(bf16[8,128,128]{2,1,0:T(8,128)(2,1)} %collective-permute-done.4.refs_1_.refs_5_), channel_id=1, source_target_pairs={{0,2},{2,4},{4,6},{6,8},{8,10},{10,12},{12,14},{14,0},{1,3},{3,5},... | collective-permute-start | bytes 786440 | tf_op jit(solution)/shard_map/ppermute | solution.py:329
  54.6 0.8 copy-start.1
  55.4 5.6 %copy-start.2 = (bf16[128,128]{1,0:T(8,128)(2,1)S(1)}, bf16[128,128]{1,0:T(8,128)(2,1)}, u32[]{:S(2)}) copy-start(bf16[128,128]{1,0:T(8,128)(2,1)} %constant.103.clone.refs_7_.refs_5_) | copy-start | bytes 98308
  58.7 8.3 %collective-permute-start.12 = (bf16[8,128,128]{2,1,0:T(8,128)(2,1)}, bf16[8,128,128]{2,1,0:T(8,128)(2,1)S(1)}, u32[]{:S(2)}, u32[]{:S(2)}) collective-permute-start(bf16[8,128,128]{2,1,0:T(8,128)(2,1)} %collective-permute-done.5.refs_0_.refs_6_), channel_id=1, source_target_pairs={{0,2},{2,4},{4,6},{6,8},{8,10},{10,12},{12,14},{14,0},{1,3},{3,5},... | collective-permute-start | bytes 786440 | tf_op jit(solution)/shard_map/ppermute | solution.py:329
  59.8 7.3 %collective-permute-start.13 = (bf16[8,128,128]{2,1,0:T(8,128)(2,1)}, bf16[8,128,128]{2,1,0:T(8,128)(2,1)S(1)}, u32[]{:S(2)}, u32[]{:S(2)}) collective-permute-start(bf16[8,128,128]{2,1,0:T(8,128)(2,1)} %collective-permute-done.9.refs_3_.refs_11_), channel_id=1, source_target_pairs={{0,14},{2,0},{4,2},{6,4},{8,6},{10,8},{12,10},{14,12},{1,15},{3,1}... | collective-permute-start | bytes 786440 | tf_op jit(solution)/shard_map/ppermute | solution.py:329
  61.0 12.8 %collective-permute-start.16 = (bf16[3,33,2,16,128]{4,3,2,1,0:T(8,128)(2,1)S(1)}, bf16[3,33,2,16,128]{4,3,2,1,0:T(8,128)(2,1)S(1)}, u32[]{:S(2)}, u32[]{:S(2)}) collective-permute-start(bf16[3,33,2,16,128]{4,3,2,1,0:T(8,128)(2,1)S(1)} %get-tuple-element.32), channel_id=1, source_target_pairs={{0,1},{1,0},{2,3},{3,2},{4,5},{5,4},{6,7},{7,6},{8,9},{9,8},{10,11... | collective-permute-start | bytes 2433032 | tf_op jit(solution)/shard_map/ppermute | solution.py:333
  63.8 10.1 %copy-start.5 = (bf16[2,33,128,128]{3,2,1,0:T(8,128)(2,1)S(1)}, bf16[2,33,128,128]{3,2,1,0:T(8,128)(2,1)}, u32[]{:S(2)}) copy-start(bf16[2,33,128,128]{3,2,1,0:T(8,128)(2,1)} %constant.109.clone.refs_6_) | copy-start | bytes 6488068
  63.8 10.0 %copy-start.6 = (bf16[256,256]{1,0:T(8,128)(2,1)S(1)}, bf16[256,256]{1,0:T(8,128)(2,1)}, u32[]{:S(2)}) copy-start(bf16[256,256]{1,0:T(8,128)(2,1)} %constant.108.clone.refs_8_) | copy-start | bytes 393220
  63.8 10.0 %copy-start.7 = (bf16[256,256]{1,0:T(8,128)(2,1)S(1)}, bf16[256,256]{1,0:T(8,128)(2,1)}, u32[]{:S(2)}) copy-start(bf16[256,256]{1,0:T(8,128)(2,1)} %constant.107.clone.refs_7_) | copy-start | bytes 393220
  70.6 3.2 %collective-permute-start.18 = (bf16[3,33,2,16,128]{4,3,2,1,0:T(8,128)(2,1)S(1)}, bf16[3,33,2,16,128]{4,3,2,1,0:T(8,128)(2,1)S(1)}, u32[]{:S(2)}, u32[]{:S(2)}) collective-permute-start(bf16[3,33,2,16,128]{4,3,2,1,0:T(8,128)(2,1)S(1)} %get-tuple-element.34), channel_id=1, source_target_pairs={{0,1},{1,0},{2,3},{3,2},{4,5},{5,4},{6,7},{7,6},{8,9},{9,8},{10,11... | collective-permute-start | bytes 2433032 | tf_op jit(solution)/shard_map/ppermute | solution.py:333
  70.7 3.1 %collective-permute-start.17 = (bf16[2,33,2,16,128]{4,3,2,1,0:T(8,128)(2,1)S(1)}, bf16[2,33,2,16,128]{4,3,2,1,0:T(8,128)(2,1)S(1)}, u32[]{:S(2)}, u32[]{:S(2)}) collective-permute-start(bf16[2,33,2,16,128]{4,3,2,1,0:T(8,128)(2,1)S(1)} %get-tuple-element.33), channel_id=1, source_target_pairs={{0,1},{1,0},{2,3},{3,2},{4,5},{5,4},{6,7},{7,6},{8,9},{9,8},{10,11... | collective-permute-start | bytes 1622024 | tf_op jit(solution)/shard_map/ppermute | solution.py:333
  73.8 10.3 %copy-start.3 = (bf16[256,256]{1,0:T(8,128)(2,1)S(1)}, bf16[256,256]{1,0:T(8,128)(2,1)}, u32[]{:S(2)}) copy-start(bf16[256,256]{1,0:T(8,128)(2,1)} %constant.106.clone.refs_19_) | copy-start | bytes 393220
  73.8 10.2 %copy-start.4 = (bf16[128,128]{1,0:T(8,128)(2,1)S(1)}, bf16[128,128]{1,0:T(8,128)(2,1)}, u32[]{:S(2)}) copy-start(bf16[128,128]{1,0:T(8,128)(2,1)} %constant.104.clone.refs_18_) | copy-start | bytes 98308
  79.7 4.3 %collective-permute-start.19 = (bf16[2,33,2,64,128]{4,3,2,1,0:T(8,128)(2,1)S(1)}, bf16[2,33,2,64,128]{4,3,2,1,0:T(8,128)(2,1)S(1)}, u32[]{:S(2)}, u32[]{:S(2)}) collective-permute-start(bf16[2,33,2,64,128]{4,3,2,1,0:T(8,128)(2,1)S(1)} %get-tuple-element.36), channel_id=1, source_target_pairs={{0,1},{1,0},{2,3},{3,2},{4,5},{5,4},{6,7},{7,6},{8,9},{9,8},{10,11... | collective-permute-start | bytes 6488072 | tf_op jit(solution)/shard_map/ppermute | solution.py:333
  126.7 8.6 %collective-permute-start.20 = (bf16[4,128,128]{2,1,0:T(8,128)(2,1)S(1)}, bf16[4,128,128]{2,1,0:T(8,128)(2,1)S(1)}, u32[]{:S(2)}, u32[]{:S(2)}) collective-permute-start(bf16[4,128,128]{2,1,0:T(8,128)(2,1)S(1)} %reduce_sum.12), channel_id=1, source_target_pairs={{4,0},{12,1},{6,2},{14,3},{8,4},{0,5},{10,6},{2,7},{5,8},{13,9},{7... | collective-permute-start | bytes 393224 | tf_op jit(solution)/shard_map/ppermute | solution.py:349
